TPU v7x, 32 devices: a whole 2x2x4 slice. The times are simulated.
32 devices in a mesh: section: 2 (over x), dp: 16 (over z, y, core).
Axes of the slice: x: 2, y: 2, z: 4, core: 2. Of those that a mesh axis runs over, the one named last changes fastest.
Arguments:
- patches: bfloat16 [32, 196, 768], P('dp'), may hold values from -6 to 6
- cotangent: bfloat16 [32, 98, 768], P('dp'), may hold values from -6 to 6
- ordering: int32 [32, 196], P('dp'), may hold values from 0 to 195, each once within a row
- lead_qkv: bfloat16 [2, 768, 2304], P('section', 'dp'), may hold values from -0.21875 to 0.21875
- lead_proj: bfloat16 [2, 768, 768], P('section', 'dp'), may hold values from -0.4375 to 0.4375
- lead_up: bfloat16 [2, 768, 3072], P('section', 'dp'), may hold values from -0.21875 to 0.21875
- lead_down: bfloat16 [2, 3072, 768], P('section', 'dp'), may hold values from -0.109375 to 0.109375
- lead_vectors: bfloat16 [2, 12, 768], P('section', None, 'dp'), may hold values from -3 to 3, as said below
- lead_bias: bfloat16 [2, 3072], P('section', 'dp'), may hold values from -1 to 1
- side_qkv: bfloat16 [2, 768, 2304], P('section', 'dp'), may hold values from -0.21875 to 0.21875
- side_proj: bfloat16 [2, 768, 768], P('section', 'dp'), may hold values from -0.4375 to 0.4375
- side_up: bfloat16 [2, 768, 3072], P('section', 'dp'), may hold values from -0.21875 to 0.21875
- side_down: bfloat16 [2, 3072, 768], P('section', 'dp'), may hold values from -0.109375 to 0.109375
- side_vectors: bfloat16 [2, 13, 768], P('section', None, 'dp'), may hold values from -3 to 3, as said below
- side_bias: bfloat16 [2, 3072], P('section', 'dp'), may hold values from -1 to 1
Outputs:
- section_rows: float32 [2, 32, 196, 768], P('section', 'dp')
- lead_qkv_grad: float32 [2, 768, 2304], P('section', 'dp')
- lead_proj_grad: float32 [2, 768, 768], P('section', 'dp')
- lead_up_grad: float32 [2, 768, 3072], P('section', 'dp')
- lead_down_grad: float32 [2, 3072, 768], P('section', 'dp')
- lead_vectors_grad: float32 [2, 12, 768], P('section', None, 'dp')
- lead_bias_grad: float32 [2, 3072], P('section', 'dp')
- decoder_qkv_grad: float32 [768, 2304], P(('section', 'dp'))
- decoder_proj_grad: float32 [768, 768], P(('section', 'dp'))
- decoder_up_grad: float32 [768, 3072], P(('section', 'dp'))
- decoder_down_grad: float32 [3072, 768], P(('section', 'dp'))
- decoder_vectors_grad: float32 [13, 768], P(None, ('section', 'dp'))
- decoder_bias_grad: float32 [3072], P(('section', 'dp'))
Inputs may be any that keep to these rules, and one draw needn't show every extreme that they name: `ordering`: each row lists every patch of one crop once; its first 98 entries are the masked patches, the remaining ones the visible patches, in the order in which the blocks take them. `lead_vectors`: gains (rows 0, 2, 4) lie near 1, layer scales (rows 10, 11) between 0.5 and 1.5. `side_vectors`: gains (rows 0, 2, 4) lie near 1, layer scales (rows 10, 11) between 0.5 and 1.5.
All inputs are finite; a program needn't handle non-finite values.
Results may differ from a plain program's by a relative error of at most 0.014.
Values may be sent and summed in bfloat16 or wider, within the bound.
A program may use at most 320 MiB of HBM per device.

v0:
```python
import jax
import jax.numpy as jnp
from jax import lax
from jax.sharding import PartitionSpec as P

D = 768
HEADS = 12
HEAD_DIM = 64
FF = 3072
GRID = 14
MICRO = 2
PATCHES = 196
MASKED = 98


def passed_along(array, axis, by):
    count = lax.axis_size(axis)
    pairs = [(i, i + by) for i in range(count) if 0 <= i + by < count]
    return lax.ppermute(array, axis, pairs)


def layer_norm(values, gain, shift):
    center = values - jnp.mean(values, axis=-1, keepdims=True)
    spread = jnp.mean(center * center, axis=-1, keepdims=True)
    return center * lax.rsqrt(spread + 1e-06) * gain + shift


def positions():
    patch_ids = jnp.arange(PATCHES)
    height = (patch_ids // GRID).astype(jnp.float32)
    across = (patch_ids % GRID).astype(jnp.float32)
    quarter = D // 4
    frequency = 1.0 / 10000.0 ** (jnp.arange(quarter).astype(jnp.float32) / quarter)
    angle_rows = height[:, None] * frequency[None, :]
    angle_cols = across[:, None] * frequency[None, :]
    return jnp.concatenate(
        [jnp.sin(angle_cols), jnp.cos(angle_cols), jnp.sin(angle_rows), jnp.cos(angle_rows)], axis=1
    )


def gelu_exact(values):
    return jax.nn.gelu(values, approximate=False)


def project(values, weight):
    return jnp.dot(values, weight, preferred_element_type=jnp.float32)


def contract_rows(left, right):
    return jnp.einsum("gli,glo->io", left, right, preferred_element_type=jnp.float32)


def back_project(grad_rows, weight):
    return jnp.einsum("glo,io->gli", grad_rows, weight, preferred_element_type=jnp.float32)


def row_total(values):
    return jnp.sum(values.astype(jnp.float32), axis=(0, 1))


def split_heads(values):
    return values.reshape(values.shape[0], values.shape[1], HEADS, HEAD_DIM)


def attend_forward(queries, key_rows, value_rows):
    scores = jnp.einsum(
        "gqhd,gkhd->ghqk",
        split_heads(queries),
        split_heads(key_rows),
        preferred_element_type=jnp.float32,
    )
    scores = scores * HEAD_DIM ** (-0.5)
    top_score = jnp.max(scores, axis=-1, keepdims=True)
    powers = jnp.exp(scores - top_score)
    total_mass = jnp.sum(powers, axis=-1, keepdims=True)
    probs = (powers / total_mass).astype(jnp.bfloat16)
    mixed_rows = jnp.einsum(
        "ghqk,gkhd->gqhd", probs, split_heads(value_rows), preferred_element_type=jnp.float32
    )
    return (
        mixed_rows.reshape(queries.shape[0], queries.shape[1], D),
        top_score + jnp.log(total_mass),
    )


def attend_backward(queries, key_rows, value_rows, log_total, grad_mixed):
    query_heads = split_heads(queries)
    key_heads = split_heads(key_rows)
    scores = jnp.einsum(
        "gqhd,gkhd->ghqk", query_heads, key_heads, preferred_element_type=jnp.float32
    )
    probs = jnp.exp(scores * HEAD_DIM ** (-0.5) - log_total)
    grad_heads = split_heads(grad_mixed)
    grad_values = jnp.einsum(
        "ghqk,gqhd->gkhd",
        probs.astype(jnp.bfloat16),
        grad_heads,
        preferred_element_type=jnp.float32,
    )
    grad_probs = jnp.einsum(
        "gqhd,gkhd->ghqk", grad_heads, split_heads(value_rows), preferred_element_type=jnp.float32
    )
    grad_scores = probs * (grad_probs - jnp.sum(grad_probs * probs, axis=-1, keepdims=True))
    grad_scores = grad_scores.astype(jnp.bfloat16)
    grad_queries = jnp.einsum(
        "ghqk,gkhd->gqhd", grad_scores, key_heads, preferred_element_type=jnp.float32
    ) * HEAD_DIM ** (-0.5)
    grad_keys = jnp.einsum(
        "ghqk,gqhd->gkhd", grad_scores, query_heads, preferred_element_type=jnp.float32
    ) * HEAD_DIM ** (-0.5)
    rows_q = queries.shape[1]
    rows_k = key_rows.shape[1]
    groups = queries.shape[0]
    return (
        grad_queries.reshape(groups, rows_q, D).astype(jnp.bfloat16),
        grad_keys.reshape(groups, rows_k, D).astype(jnp.bfloat16),
        grad_values.reshape(groups, rows_k, D).astype(jnp.bfloat16),
    )


def run_block(stream, context, weights):
    qkv_weight, proj_weight, up_weight, down_weight, vectors, up_bias = weights
    rows_q = stream.shape[1]
    source = stream if context is None else jnp.concatenate([context, stream], axis=1)
    normed, first_back = jax.vjp(layer_norm, source, vectors[0], vectors[1])
    normed_low = normed.astype(jnp.bfloat16)
    if context is None:
        combined = project(normed_low, qkv_weight)
        queries = combined[..., :D] + vectors[6]
        key_rows = combined[..., D : 2 * D]
        value_rows = combined[..., 2 * D :] + vectors[7]
    else:
        queries = project(normed_low[:, -rows_q:], qkv_weight[:, :D]) + vectors[6]
        pair_rows = project(normed_low, qkv_weight[:, D:])
        key_rows = pair_rows[..., :D]
        value_rows = pair_rows[..., D:] + vectors[7]
    queries = queries.astype(jnp.bfloat16)
    key_rows = key_rows.astype(jnp.bfloat16)
    value_rows = value_rows.astype(jnp.bfloat16)
    mixed_rows, log_total = attend_forward(queries, key_rows, value_rows)
    mixed_low = mixed_rows.astype(jnp.bfloat16)
    attn_out = project(mixed_low, proj_weight) + vectors[8]
    residual = stream + vectors[10] * attn_out
    second, second_back = jax.vjp(layer_norm, residual, vectors[2], vectors[3])
    second_low = second.astype(jnp.bfloat16)
    pre_gelu = project(second_low, up_weight) + up_bias
    hidden, gelu_back = jax.vjp(gelu_exact, pre_gelu)
    hidden_low = hidden.astype(jnp.bfloat16)
    branch = project(hidden_low, down_weight) + vectors[9]
    output, final_back = jax.vjp(
        layer_norm, residual + vectors[11] * branch, vectors[4], vectors[5]
    )

    def backward(grad_out):
        grad_final, grad_final_gain, grad_final_shift = final_back(grad_out)
        grad_scale_two = row_total(grad_final * branch)
        grad_branch = (vectors[11] * grad_final).astype(jnp.bfloat16)
        grad_hidden = back_project(grad_branch, down_weight)
        (grad_pre,) = gelu_back(grad_hidden)
        grad_pre = grad_pre.astype(jnp.bfloat16)
        grad_second = back_project(grad_pre, up_weight)
        grad_resid, grad_gain_two, grad_shift_two = second_back(grad_second)
        grad_resid = grad_resid + grad_final
        grad_scale_one = row_total(grad_resid * attn_out)
        grad_attn = (vectors[10] * grad_resid).astype(jnp.bfloat16)
        grad_mixed = back_project(grad_attn, proj_weight).astype(jnp.bfloat16)
        grad_queries, grad_keys, grad_values = attend_backward(
            queries, key_rows, value_rows, log_total, grad_mixed
        )
        tail_rows = ((mixed_low, grad_attn), (second_low, grad_pre), (hidden_low, grad_branch))
        if context is None:
            grad_joined = jnp.concatenate([grad_queries, grad_keys, grad_values], axis=-1)
            grad_normed = back_project(grad_joined, qkv_weight)
            pairs = ((normed_low, grad_joined),) + tail_rows
        else:
            grad_pair = jnp.concatenate([grad_keys, grad_values], axis=-1)
            grad_normed = back_project(grad_pair, qkv_weight[:, D:])
            grad_query_rows = back_project(grad_queries, qkv_weight[:, :D])
            grad_normed = jnp.concatenate(
                [grad_normed[:, :-rows_q], grad_normed[:, -rows_q:] + grad_query_rows], axis=1
            )
            pairs = ((normed_low[:, -rows_q:], grad_queries), (normed_low, grad_pair)) + tail_rows
        grad_source, grad_gain_one, grad_shift_one = first_back(grad_normed)
        grad_vectors = jnp.stack(
            [
                grad_gain_one,
                grad_shift_one,
                grad_gain_two,
                grad_shift_two,
                grad_final_gain,
                grad_final_shift,
                row_total(grad_queries),
                row_total(grad_values),
                row_total(grad_attn),
                row_total(grad_branch),
                grad_scale_one,
                grad_scale_two,
            ]
        )
        grad_bias = row_total(grad_pre)
        if context is None:
            grad_stream = grad_resid + grad_source
            grad_context = None
        else:
            grad_stream = grad_resid + grad_source[:, -rows_q:]
            grad_context = grad_source[:, :-rows_q]
        return (grad_stream, grad_context, pairs, (grad_vectors, grad_bias))

    return (output, backward)


def empty_pairs(count, rows_q, rows_k, cross):

    def blank(rows, width):
        return jnp.zeros((count, rows, width), jnp.bfloat16)

    if cross:
        first = ((blank(rows_q, D), blank(rows_q, D)), (blank(rows_k, D), blank(rows_k, 2 * D)))
    else:
        first = ((blank(rows_q, D), blank(rows_q, 3 * D)),)
    return first + (
        (blank(rows_q, D), blank(rows_q, D)),
        (blank(rows_q, D), blank(rows_q, FF)),
        (blank(rows_q, FF), blank(rows_q, D)),
    )


def empty_small(row_count):
    return (jnp.zeros((row_count, D), jnp.float32), jnp.zeros((FF,), jnp.float32))


def weight_grads(pairs, cross):
    if cross:
        grad_qkv = jnp.concatenate([contract_rows(*pairs[0]), contract_rows(*pairs[1])], axis=1)
        rest = pairs[2:]
    else:
        grad_qkv = contract_rows(*pairs[0])
        rest = pairs[1:]
    return (grad_qkv, contract_rows(*rest[0]), contract_rows(*rest[1]), contract_rows(*rest[2]))


def join_micro(collected):
    return jax.tree.map(lambda *pieces: jnp.concatenate(pieces, axis=0), *collected)


def add_micro(collected):
    return jax.tree.map(lambda *pieces: sum(pieces[1:], pieces[0]), *collected)


def encode(patch_part, order_part, lead_set, side_set):
    visible = jnp.take_along_axis(patch_part, order_part[:, MASKED:, None], axis=1).astype(
        jnp.float32
    )
    masked = jnp.take_along_axis(patch_part, order_part[:, :MASKED, None], axis=1).astype(
        jnp.float32
    )
    latents, unused_back = run_block(visible, None, lead_set)
    targets, unused_teacher = run_block(masked, None, side_set)
    return jnp.stack([latents.astype(jnp.bfloat16), targets.astype(jnp.bfloat16)])


def encode_back(patch_part, order_part, grad_latents, lead_set):
    visible = jnp.take_along_axis(patch_part, order_part[:, MASKED:, None], axis=1).astype(
        jnp.float32
    )
    unused_out, backward = run_block(visible, None, lead_set)
    grad_rows, unused_context, pairs, small = backward(grad_latents.astype(jnp.float32))
    crop_ids = lax.broadcasted_iota(jnp.int32, (patch_part.shape[0], 1), 0)
    grad_in = (
        jnp.zeros(patch_part.shape, jnp.float32).at[crop_ids, order_part[:, MASKED:]].set(grad_rows)
    )
    return (pairs, small, grad_in)


def regress(latent_pack, order_part, cot_part, lead_set, side_set):
    pos_table = positions()
    pos_visible = jnp.take(pos_table, order_part[:, MASKED:], axis=0)
    pos_masked = jnp.take(pos_table, order_part[:, :MASKED], axis=0)
    mask_queries = side_set[4][12] + pos_masked
    latents = latent_pack[0].astype(jnp.float32)
    targets = latent_pack[1].astype(jnp.float32)
    regressed, regress_back = run_block(mask_queries, latents + pos_visible, lead_set)
    decoded, decode_back = run_block(regressed + pos_masked, None, side_set)
    grad_decode_in, unused_context, dec_pairs, dec_small = decode_back(cot_part.astype(jnp.float32))
    grad_queries, grad_latents, reg_pairs, reg_small = regress_back(
        grad_decode_in + regressed - targets
    )
    dec_small = (
        jnp.concatenate([dec_small[0], row_total(grad_queries)[None]], axis=0),
        dec_small[1],
    )
    return (
        grad_latents.astype(jnp.bfloat16),
        jnp.concatenate([regressed, decoded], axis=1),
        reg_pairs,
        reg_small,
        dec_pairs,
        dec_small,
    )


def lead_view(member, count, column_kind):
    if column_kind:
        return member.T.reshape(count, -1)
    return member.reshape(count, -1)


def side_view(member, count, column_kind):
    if column_kind:
        return member.T.reshape(2, count, -1)
    return member.reshape(2, count, -1)


def lead_unview(piece, shape, count, column_kind):
    if column_kind:
        return piece.reshape(shape[1] // count, shape[0]).T
    return piece.reshape((shape[0] // count,) + tuple(shape[1:]))


def pack_rows(views, count):
    flat = jnp.concatenate(views, axis=1)
    width = flat.shape[1]
    padded = -(-width // 1024) * 1024
    flat = jnp.pad(flat, ((0, 0), (0, padded - width)))
    return (flat.reshape(count * 8, padded // 8), width)


def split_flat(flat, widths):
    pieces = []
    offset = 0
    for width in widths:
        pieces.append(flat[offset : offset + width])
        offset = offset + width
    return pieces


def shards(
    patches,
    cotangent,
    ordering,
    lead_qkv,
    lead_proj,
    lead_up,
    lead_down,
    lead_vectors,
    lead_bias,
    side_qkv,
    side_proj,
    side_up,
    side_down,
    side_vectors,
    side_bias,
):
    section_id = lax.axis_index("section")
    on_encoder = section_id == 0
    count = lax.axis_size("dp")
    fetched = (
        lax.all_gather(lead_qkv, "dp", axis=1, tiled=True),
        lax.all_gather(lead_proj, "dp", axis=1, tiled=True),
        lax.all_gather(lead_up, "dp", axis=1, tiled=True),
        lax.all_gather(lead_down, "dp", axis=1, tiled=True),
        lax.all_gather(lead_vectors, "dp", axis=2, tiled=True),
        lax.all_gather(lead_bias, "dp", axis=1, tiled=True),
        lax.all_gather(side_qkv, "dp", axis=1, tiled=True),
        lax.all_gather(side_proj, "dp", axis=1, tiled=True),
        lax.all_gather(side_up, "dp", axis=1, tiled=True),
        lax.all_gather(side_down, "dp", axis=1, tiled=True),
        lax.all_gather(side_vectors, "dp", axis=2, tiled=True),
        lax.all_gather(side_bias, "dp", axis=1, tiled=True),
    )
    lead_set = (
        fetched[0][0],
        fetched[1][0],
        fetched[2][0],
        fetched[3][0],
        fetched[4][0].astype(jnp.float32),
        fetched[5][0].astype(jnp.float32),
    )
    side_set = (
        fetched[6][0],
        fetched[7][0],
        fetched[8][0],
        fetched[9][0],
        fetched[10][0].astype(jnp.float32),
        fetched[11][0].astype(jnp.float32),
    )
    crops_part = patches.shape[0] // MICRO
    visible_count = PATCHES - MASKED
    rows_out = [jnp.zeros((crops_part, PATCHES, D), jnp.float32) for micro_id in range(MICRO)]
    arrived = [None] * MICRO
    returned = [None] * MICRO
    enc_pairs = [None] * MICRO
    enc_small = [None] * MICRO
    reg_pairs = [None] * MICRO
    reg_small = [None] * MICRO
    dec_pairs = [None] * MICRO
    dec_small = [None] * MICRO
    for phase_id in range(MICRO + 2):
        if phase_id < MICRO:
            lower = phase_id * crops_part
            latent_pack = lax.cond(
                on_encoder,
                lambda: encode(
                    patches[lower : lower + crops_part],
                    ordering[lower : lower + crops_part],
                    lead_set,
                    side_set,
                ),
                lambda: jnp.zeros((2, crops_part, MASKED, D), jnp.bfloat16),
            )
        if phase_id >= 2:
            finished = phase_id - 2
            lower_done = finished * crops_part
            enc_pairs[finished], enc_small[finished], rows_out[finished] = lax.cond(
                on_encoder,
                lambda: encode_back(
                    patches[lower_done : lower_done + crops_part],
                    ordering[lower_done : lower_done + crops_part],
                    returned[finished],
                    lead_set,
                ),
                lambda: (
                    empty_pairs(crops_part, visible_count, visible_count, False),
                    empty_small(12),
                    rows_out[finished],
                ),
            )
        if 1 <= phase_id <= MICRO:
            current = phase_id - 1
            lower_now = current * crops_part
            (
                grad_pack,
                rows_out[current],
                reg_pairs[current],
                reg_small[current],
                dec_pairs[current],
                dec_small[current],
            ) = lax.cond(
                on_encoder,
                lambda: (
                    jnp.zeros((crops_part, visible_count, D), jnp.bfloat16),
                    rows_out[current],
                    empty_pairs(crops_part, MASKED, PATCHES, True),
                    empty_small(12),
                    empty_pairs(crops_part, MASKED, MASKED, False),
                    empty_small(13),
                ),
                lambda: regress(
                    arrived[current],
                    ordering[lower_now : lower_now + crops_part],
                    cotangent[lower_now : lower_now + crops_part],
                    lead_set,
                    side_set,
                ),
            )
        if phase_id < MICRO:
            arrived[phase_id] = passed_along(latent_pack, "section", 1)
        if 1 <= phase_id <= MICRO:
            returned[current] = passed_along(grad_pack, "section", -1)
    enc_all = join_micro(enc_pairs)
    reg_all = join_micro(reg_pairs)
    dec_all = join_micro(dec_pairs)
    lead_big = lax.cond(
        on_encoder, lambda: weight_grads(enc_all, False), lambda: weight_grads(reg_all, True)
    )
    lead_small = add_micro(enc_small + reg_small)
    side_big = lax.cond(
        on_encoder,
        lambda: tuple((jnp.zeros(member.shape, jnp.float32) for member in side_set[:4])),
        lambda: weight_grads(dec_all, False),
    )
    side_small_sum = add_micro(dec_small)
    grads_lead = lead_big + lead_small
    grads_side = side_big + side_small_sum
    column_kinds = (False, False, False, False, True, False)
    lead_views = [lead_view(member, count, kind) for member, kind in zip(grads_lead, column_kinds)]
    side_views = [side_view(member, count, kind) for member, kind in zip(grads_side, column_kinds)]
    lead_widths = [view.shape[1] for view in lead_views]
    side_widths = [view.shape[2] for view in side_views]
    lead_total = sum(lead_widths)
    side_total = sum(side_widths)
    packed, width = pack_rows(
        lead_views + [view[0] for view in side_views] + [view[1] for view in side_views], count
    )
    reduced = lax.psum_scatter(packed, "dp", scatter_dimension=0, tiled=True).reshape(-1)[:width]
    lead_flat = reduced[:lead_total]
    first_flat = reduced[lead_total : lead_total + side_total]
    second_flat = reduced[lead_total + side_total :]
    received = passed_along(first_flat.astype(jnp.bfloat16), "section", -1).astype(first_flat.dtype)
    side_flat = jnp.where(on_encoder, received, second_flat)
    lead_pieces = split_flat(lead_flat, lead_widths)
    side_pieces = split_flat(side_flat, side_widths)
    lead_out = [
        lead_unview(piece, member.shape, count, kind)
        for piece, member, kind in zip(lead_pieces, grads_lead, column_kinds)
    ]
    side_out = [
        lead_unview(piece, member.shape, 2 * count, kind)
        for piece, member, kind in zip(side_pieces, grads_side, column_kinds)
    ]
    section_rows = jnp.concatenate(rows_out, axis=0)[None]
    return (
        section_rows,
        lead_out[0][None],
        lead_out[1][None],
        lead_out[2][None],
        lead_out[3][None],
        lead_out[4][None],
        lead_out[5][None],
        side_out[0],
        side_out[1],
        side_out[2],
        side_out[3],
        side_out[4],
        side_out[5],
    )


def solution(mesh):
    return jax.shard_map(
        shards,
        mesh=mesh,
        in_specs=(
            P("dp", None, None),
            P("dp", None, None),
            P("dp", None),
            P("section", "dp", None),
            P("section", "dp", None),
            P("section", "dp", None),
            P("section", "dp", None),
            P("section", None, "dp"),
            P("section", "dp"),
            P("section", "dp", None),
            P("section", "dp", None),
            P("section", "dp", None),
            P("section", "dp", None),
            P("section", None, "dp"),
            P("section", "dp"),
        ),
        out_specs=(
            P("section", "dp", None, None),
            P("section", "dp", None),
            P("section", "dp", None),
            P("section", "dp", None),
            P("section", "dp", None),
            P("section", None, "dp"),
            P("section", "dp"),
            P(("section", "dp"), None),
            P(("section", "dp"), None),
            P(("section", "dp"), None),
            P(("section", "dp"), None),
            P(None, ("section", "dp")),
            P(("section", "dp")),
        ),
        check_vma=False,
    )
```

profile of v0, /device:TPU:3, one launch (start us, length us, event | category | flops | bytes accessed | tf_op | source)
XLA Modules:
  0.0 2077.2 jit_solution(5882751501022518066)
XLA Ops:
  12.9 23.3 %all_gather.36 = bf16[1,12,768]{1,0,2:T(2,128)(2,1)S(1)} all-gather(bf16[1,12,48]{1,0,2:T(2,128)(2,1)S(1)} %copy.299), channel_id=1, replica_groups=mesh['section'=2,'dp'=16] {'dp'}, dimensions={2}, use_global_device_ids=true | all-gather | bytes 19584 | tf_op jit(solution)/shard_map/all_gather | solution.py:362
  39.2 53.1 %all-reduce.6 = (bf16[3072]{0:T(1024)(128)(2,1)S(1)}, bf16[3072]{0:T(1024)(128)(2,1)S(1)}) all-reduce(bf16[3072]{0:T(1024)(128)(2,1)S(1)} %dynamic-update-slice, bf16[3072]{0:T(1024)(128)(2,1)S(1)} %dynamic-update-slice.1), channel_id=1, replica_groups=mesh['section'=2,'dp'=16] {'dp'}, use_global_device_ids=true, to_apply=%add.3 | all-reduce | flops 6144 | bytes 24576
  93.0 23.7 %all_gather.42 = bf16[1,13,768]{1,0,2:T(2,128)(2,1)S(1)} all-gather(bf16[1,13,48]{1,0,2:T(2,128)(2,1)S(1)} %copy.300), channel_id=1, replica_groups=mesh['section'=2,'dp'=16] {'dp'}, dimensions={2}, use_global_device_ids=true | all-gather | bytes 21216 | tf_op jit(solution)/shard_map/all_gather | solution.py:368
  118.5 20.7 all-gather.9.cloned.1.call-done
  139.1 48.4 %all-gather.17.cloned.1.call-done = bf16[1,768,2304]{2,1,0:T(8,128)(2,1)} async-done(((bf16[1,48,2304]{2,1,0:T(8,128)(2,1)}), bf16[1,768,2304]{2,1,0:T(8,128)(2,1)}) %all-gather.17.cloned.1.call-update) | async-done | bytes 3538960 | tf_op jit(solution)/shard_map/all_gather | solution.py:364
  187.5 54.6 %all-gather.13.cloned.1.call-done = bf16[1,768,3072]{2,1,0:T(8,128)(2,1)} async-done(((bf16[1,48,3072]{2,1,0:T(8,128)(2,1)}), bf16[1,768,3072]{2,1,0:T(8,128)(2,1)}) %all-gather.13.cloned.1.call-update) | async-done | bytes 4718608 | tf_op jit(solution)/shard_map/all_gather | solution.py:360
  242.1 54.1 %all-gather.15.cloned.1.call-done = bf16[1,3072,768]{2,1,0:T(8,128)(2,1)} async-done(((bf16[1,192,768]{2,1,0:T(8,128)(2,1)}), bf16[1,3072,768]{2,1,0:T(8,128)(2,1)}) %all-gather.15.cloned.1.call-update) | async-done | bytes 4718608 | tf_op jit(solution)/shard_map/all_gather | solution.py:361
  296.2 54.3 %all-gather.21.cloned.1.call-done = bf16[1,768,3072]{2,1,0:T(8,128)(2,1)} async-done(((bf16[1,48,3072]{2,1,0:T(8,128)(2,1)}), bf16[1,768,3072]{2,1,0:T(8,128)(2,1)}) %all-gather.21.cloned.1.call-update) | async-done | bytes 4718608 | tf_op jit(solution)/shard_map/all_gather | solution.py:366
  350.4 54.3 %all-gather.23.cloned.1.call-done = bf16[1,3072,768]{2,1,0:T(8,128)(2,1)} async-done(((bf16[1,192,768]{2,1,0:T(8,128)(2,1)}), bf16[1,3072,768]{2,1,0:T(8,128)(2,1)}) %all-gather.23.cloned.1.call-update) | async-done | bytes 4718608 | tf_op jit(solution)/shard_map/all_gather | solution.py:367
  426.9 48.5 %collective-permute-done.2 = bf16[2,1,98,768]{3,2,1,0:T(8,128)(2,1)} collective-permute-done((bf16[2,1,98,768]{3,2,1,0:T(8,128)(2,1)}, bf16[2,1,98,768]{3,2,1,0:T(8,128)(2,1)}, u32[]{:S(2)}, u32[]{:S(2)}) %collective-permute-start.2) | collective-permute-done | bytes 301088 | tf_op jit(solution)/shard_map/ppermute | solution.py:19
  475.4 133.8 %conditional.12 = (bf16[1,98,768]{2,1,0:T(8,128)(2,1)}, bf16[1,98,768]{2,1,0:T(8,128)(2,1)}, bf16[1,196,768]{2,1,0:T(8,128)(2,1)}, bf16[1,196,1536]{1,2,0:T(8,12...) conditional(s32[]{:T(128)} %convert_element_type.1384, ...), branch_computations={%region_127.188_spmd, %region_186.189_spmd} | conditional | flops 6393245696 | bytes 351442560 | solution.py:438
  525.6 15.1 slice.1282
  611.3 125.0 %conditional.9 = (bf16[1,98,768]{2,1,0:T(8,128)(2,1)}, bf16[1,98,768]{2,1,0:T(8,128)(2,1)}, bf16[1,196,768]{2,1,0:T(8,128)(2,1)}, bf16[1,196,1536]{1,2,0:T(8,128...) conditional(s32[]{:T(128)} %convert_element_type.1384, ...), branch_computations={%region_18.79_spmd, %region_77.80_spmd} | conditional | flops 6393245696 | bytes 353267616 | solution.py:438
  759.5 64.4 %conditional.15 = (f32[16,55296]{1,0:T(8,128)}, f32[16,55296]{1,0:T(8,128)}, f32[16,18432]{1,0:T(8,128)}, f32[16,18432]{1,0:T(8,128)}, f32[16,73728]{1,0:T(8,128...) conditional(s32[]{:T(128)} %convert_element_type.1384, ...), branch_computations={%region_220.223_spmd, %region_221.224_spmd} | conditional | flops 2774532096 | bytes 147578976 | solution.py:467
  833.2 13.0 conditional.10
  857.0 56.7 %conditional.14 = (f32[16,110592]{1,0:T(8,128)}, f32[16,36864]{1,0:T(8,128)S(1)}, f32[16,147456]{1,0:T(8,128)}, f32[16,147456]{1,0:T(8,128)}) conditional(s32[]{:T(128)} %convert_element_type.1384, (bf16[2,98,768]{2,1,0:T(8,128)(2,1)S(1)}, bf16[2,98,768]{2,1,0:T(8,128)(2,1)S(1)}, bf16[2,196,768]{2,1,0:T(8,128)(2,1)S(1)}, ...), branch_computations={%region_218.221_spmd, %region_219.222_spmd} | conditional | flops 3238723584 | bytes 107520088 | solution.py:463
  878.2 10.7 reshape.5571
  895.3 10.6 reshape.5572
  953.4 10.2 dynamic-update-slice.14
  968.9 15.0 dynamic-update-slice.16
  983.8 14.6 dynamic-update-slice.17
  1001.4 37.3 %pad.6 = f32[16,886784]{1,0:T(8,128)} pad(f32[16,886320]{1,0:T(8,128)} %dynamic-update-slice.19, f32[]{:T(128)} %constant.674.clone.1), padding=0_0x0_464 | pad | bytes 113478656 | tf_op jit(solution)/shard_map/jit(_pad)/pad | solution.py:324
  1038.7 76.0 %reshape.5589 = f32[128,110848]{1,0:T(8,128)} reshape(f32[16,886784]{1,0:T(8,128)} %pad.6) | data formatting | bytes 113508352 | tf_op jit(solution)/shard_map/reshape | solution.py:325
  1119.2 923.4 %all-reduce.9.cloned.1.call-done = f32[128,110848]{1,0:T(8,128)} async-done(((f32[128,110848]{1,0:T(8,128)}), f32[128,110848]{1,0:T(8,128)}) %all-reduce.9.cloned.1.call-update) | async-done | bytes 56754192
  (1259 shorter events, 481.1 us)
Async XLA Ops:
  7.2 111.3 %all-gather.11.cloned.1.call-start = ((), (), s32[]{:S(2)}) async-start(), calls=%async_computation.1 | async-start | bytes 1253376 | tf_op jit(solution)/shard_map/all_gather | solution.py:359
  7.9 110.6 %all-gather.19.cloned.1.call-start = ((), (), s32[]{:S(2)}) async-start(), calls=%async_computation.5 | async-start | bytes 1253376 | tf_op jit(solution)/shard_map/all_gather | solution.py:365
  8.7 130.5 %all-gather.9.cloned.1.call-start = ((), (), s32[]{:S(2)}) async-start(), calls=%async_computation | async-start | bytes 3760128 | tf_op jit(solution)/shard_map/all_gather | solution.py:358
  9.4 27.9 %copy-start.431 = (bf16[1,192]{1,0:T(2,128)(2,1)S(1)}, bf16[1,192]{1,0:T(2,128)(2,1)}, u32[]{:S(2)}) copy-start(bf16[1,192]{1,0:T(2,128)(2,1)} %param.43) | copy-start | bytes 1156
  9.4 27.9 %copy-start.432 = (bf16[1,192]{1,0:T(2,128)(2,1)S(1)}, bf16[1,192]{1,0:T(2,128)(2,1)}, u32[]{:S(2)}) copy-start(bf16[1,192]{1,0:T(2,128)(2,1)} %param.49) | copy-start | bytes 1156
  9.4 178.1 %all-gather.17.cloned.1.call-start = ((), (), s32[]{:S(2)}) async-start(), calls=%async_computation.4 | async-start | bytes 3760128 | tf_op jit(solution)/shard_map/all_gather | solution.py:364
  10.0 27.4 %copy-start.430 = (u32[32]{0:T(128)S(1)}, u32[32]{0:T(128)}, u32[]{:S(2)}) copy-start(u32[32]{0:T(128)} %constant.702) | copy-start | bytes 388
  10.0 82.9 %copy-start.419 = (bf16[1,13,48]{2,1,0:T(8,128)(2,1)S(1)}, bf16[1,13,48]{2,1,0:T(8,128)(2,1)}, u32[]{:S(2)}) copy-start(bf16[1,13,48]{2,1,0:T(8,128)(2,1)} %param.48) | copy-start | bytes 3748
  10.0 232.0 %all-gather.13.cloned.1.call-start = ((), (), s32[]{:S(2)}) async-start(), calls=%async_computation.2 | async-start | bytes 5013504 | tf_op jit(solution)/shard_map/all_gather | solution.py:360
  10.6 285.6 %all-gather.15.cloned.1.call-start = ((), (), s32[]{:S(2)}) async-start(), calls=%async_computation.3 | async-start | bytes 5013504 | tf_op jit(solution)/shard_map/all_gather | solution.py:361
  11.2 339.2 %all-gather.21.cloned.1.call-start = ((), (), s32[]{:S(2)}) async-start(), calls=%async_computation.6 | async-start | bytes 5013504 | tf_op jit(solution)/shard_map/all_gather | solution.py:366
  11.9 392.7 %all-gather.23.cloned.1.call-start = ((), (), s32[]{:S(2)}) async-start(), calls=%async_computation.7 | async-start | bytes 5013504 | tf_op jit(solution)/shard_map/all_gather | solution.py:367
  12.7 2029.9 %all-reduce.9.cloned.1.call-start = ((), (), s32[]{:S(2)}) async-start(), calls=%async_computation.8 | async-start | bytes 113508352
  12.9 391.8 %copy-start.298 = (s32[2,196]{1,0:T(2,128)S(1)}, s32[2,196]{1,0:T(2,128)}, u32[]{:S(2)}) copy-start(s32[2,196]{1,0:T(2,128)} %param.37) | copy-start | bytes 4708
  414.3 61.1 %collective-permute-start.2 = (bf16[2,1,98,768]{3,2,1,0:T(8,128)(2,1)}, bf16[2,1,98,768]{3,2,1,0:T(8,128)(2,1)}, u32[]{:S(2)}, u32[]{:S(2)}) collective-permute-start(bf16[2,1,98,768]{3,2,1,0:T(8,128)(2,1)} %get-tuple-element.1662), channel_id=1, source_target_pairs={{0,16},{1,17},{2,18},{3,19},{4,20},{5,21},{6,22},{7,23},{8,24},{9,... | collective-permute-start | bytes 903176 | tf_op jit(solution)/shard_map/ppermute | solution.py:19
  425.6 185.6 %collective-permute-start = (bf16[2,1,98,768]{3,2,1,0:T(8,128)(2,1)}, bf16[2,1,98,768]{3,2,1,0:T(8,128)(2,1)}, u32[]{:S(2)}, u32[]{:S(2)}) collective-permute-start(bf16[2,1,98,768]{3,2,1,0:T(8,128)(2,1)} %get-tuple-element.1661), channel_id=1, source_target_pairs={{0,16},{1,17},{2,18},{3,19},{4,20},{5,21},{6,22},{7,23},{8,24},{9,... | collective-permute-start | bytes 903176 | tf_op jit(solution)/shard_map/ppermute | solution.py:19
  609.3 216.8 %collective-permute-start.3 = (bf16[1,98,768]{2,1,0:T(8,128)(2,1)}, bf16[1,98,768]{2,1,0:T(8,128)(2,1)}, u32[]{:S(2)}, u32[]{:S(2)}) collective-permute-start(bf16[1,98,768]{2,1,0:T(8,128)(2,1)} %get-tuple-element.461), channel_id=1, source_target_pairs={{16,0},{17,1},{18,2},{19,3},{20,4},{21,5},{22,6},{23,7},{24,8},{25... | collective-permute-start | bytes 451592 | tf_op jit(solution)/shard_map/ppermute | solution.py:19
  719.8 14.7 copy-start.97
  736.3 96.2 %collective-permute-start.1 = (bf16[1,98,768]{2,1,0:T(8,128)(2,1)}, bf16[1,98,768]{2,1,0:T(8,128)(2,1)}, u32[]{:S(2)}, u32[]{:S(2)}) collective-permute-start(bf16[1,98,768]{2,1,0:T(8,128)(2,1)} %get-tuple-element.458), channel_id=1, source_target_pairs={{16,0},{17,1},{18,2},{19,3},{20,4},{21,5},{22,6},{23,7},{24,8},{25... | collective-permute-start | bytes 451592 | tf_op jit(solution)/shard_map/ppermute | solution.py:19
  759.5 66.6 %copy-start.35 = (f32[1,12,768]{1,0,2:T(1,128)S(1)}, f32[1,12,768]{1,0,2:T(1,128)}, u32[]{:S(2)}) copy-start(f32[1,12,768]{1,0,2:T(1,128)} %convert_element_type.1398) | copy-start | bytes 110596
  759.5 66.6 %copy-start.57 = (bf16[2,196,768]{2,0,1:T(2,128)(2,1)S(1)}, bf16[2,196,768]{2,0,1:T(2,128)(2,1)}, u32[]{:S(2)}) copy-start(bf16[2,196,768]{2,0,1:T(2,128)(2,1)} %param.35) | copy-start | bytes 1806340
  983.8 14.6 copy-start.253
  983.8 16.1 copy-start.296
  2049.0 15.6 collective-permute-start.4
  (372 other events, 1214.9 us)
Sparse Core Ops, SparseCore 0:
  10.3 40.2 all-gather.10
  52.8 37.2 all-gather.18
  92.4 46.6 all-gather.8
  141.3 46.1 all-gather.16
  189.6 52.3 all-gather.12
  244.2 51.9 all-gather.14
  298.4 51.9 all-gather.20
  352.7 51.9 all-gather.22
  1114.9 927.6 all-reduce.8
where the time goes:
time: 2080 us
  waiting for transfers between devices  1260 us (61%)
  local copies, waits for them, and re-layouts  423 us (20%)
  matrix products  123 us (6%)
  blocking collectives  100 us (5%)
  other arithmetic  84.1 us (4%)
  loops' own time  58 us (3%)
    unnamed x10, waiting for transfers between devices  928 us
    unnamed x211, local copies, waits for them, and re-layouts  92.6 us
    reshape x1, local copies, waits for them, and re-layouts, pack_rows(): return (flat.reshape(count * 8, padded // 8), width)  76 us
    all_gather x1, waiting for transfers between devices, shards(): lax.all_gather(lead_up, 'dp', axis=1, tiled=True)  54.6 us
    all_gather x1, waiting for transfers between devices, shards(): lax.all_gather(side_up, 'dp', axis=1, tiled=True)  54.3 us
    all_gather x1, waiting for transfers between devices, shards(): lax.all_gather(side_down, 'dp', axis=1, tiled=True)  54.3 us
    all_gather x1, waiting for transfers between devices, shards(): lax.all_gather(lead_down, 'dp', axis=1, tiled=True)  54.1 us
    unnamed x1, blocking collectives  53.1 us
  transfers between devices with their start and end apart: 14, of which 8 were waited for; matrix products, arithmetic and copies ran while one was open for 16% of the time, Pallas kernels for 0%

commit v1 on v0

--- a/solution.py
+++ b/solution.py
@@ -1,4 +1,8 @@
+import functools
+
 import jax
+import jax.experimental.pallas as pl
+import jax.experimental.pallas.tpu as pltpu
 import jax.numpy as jnp
 from jax import lax
 from jax.sharding import PartitionSpec as P
@@ -8,7 +12,6 @@
 HEAD_DIM = 64
 FF = 3072
 GRID = 14
-MICRO = 2
 PATCHES = 196
 MASKED = 98
 
@@ -239,14 +242,6 @@
     return (grad_qkv, contract_rows(*rest[0]), contract_rows(*rest[1]), contract_rows(*rest[2]))
 
 
-def join_micro(collected):
-    return jax.tree.map(lambda *pieces: jnp.concatenate(pieces, axis=0), *collected)
-
-
-def add_micro(collected):
-    return jax.tree.map(lambda *pieces: sum(pieces[1:], pieces[0]), *collected)
-
-
 def encode(patch_part, order_part, lead_set, side_set):
     visible = jnp.take_along_axis(patch_part, order_part[:, MASKED:, None], axis=1).astype(
         jnp.float32
@@ -299,39 +294,463 @@
     )
 
 
-def lead_view(member, count, column_kind):
-    if column_kind:
-        return member.T.reshape(count, -1)
-    return member.reshape(count, -1)
-
-
-def side_view(member, count, column_kind):
-    if column_kind:
-        return member.T.reshape(2, count, -1)
-    return member.reshape(2, count, -1)
-
-
-def lead_unview(piece, shape, count, column_kind):
-    if column_kind:
-        return piece.reshape(shape[1] // count, shape[0]).T
-    return piece.reshape((shape[0] // count,) + tuple(shape[1:]))
-
-
-def pack_rows(views, count):
-    flat = jnp.concatenate(views, axis=1)
-    width = flat.shape[1]
-    padded = -(-width // 1024) * 1024
-    flat = jnp.pad(flat, ((0, 0), (0, padded - width)))
-    return (flat.reshape(count * 8, padded // 8), width)
-
-
-def split_flat(flat, widths):
-    pieces = []
-    offset = 0
-    for width in widths:
-        pieces.append(flat[offset : offset + width])
-        offset = offset + width
-    return pieces
+MESH_ID = pl.DeviceIdType.MESH
+
+
+def each(count, body):
+    if count <= 4:
+        for k in range(count):
+            body(k)
+    else:
+        lax.fori_loop(0, count, lambda k, carry: (body(k), carry)[1], 0)
+
+
+def place():
+    section = lax.axis_index("section")
+    index = lax.axis_index("dp")
+    return section, index, index // 4, (index // 2) % 2, index % 2
+
+
+def slot(outer, mid, core):
+    return outer * 4 + mid * 2 + core
+
+
+def remote(src, dst, send_sem, recv_sem, device):
+    return pltpu.make_async_remote_copy(
+        src_ref=src,
+        dst_ref=dst,
+        send_sem=send_sem,
+        recv_sem=recv_sem,
+        device_id=device,
+        device_id_type=MESH_ID,
+    )
+
+
+def greet(devices):
+    barrier = pltpu.get_barrier_semaphore()
+    for device in devices:
+        pl.semaphore_signal(barrier, inc=1, device_id=device, device_id_type=MESH_ID)
+
+
+def gather_kernel(count, groups, *refs):
+    shards_in = refs[:count]
+    wholes = refs[count : 2 * count]
+    own_sem, z_send, z_recv, y_send, y_recv, c_send, c_recv = refs[2 * count :]
+    section, index, outer, mid, core = place()
+    mid_device = (section, slot(outer, 1 - mid, core))
+    core_device = (section, slot(outer, mid, 1 - core))
+
+    def outer_device(k):
+        return (section, slot((outer + k) % groups, mid, core))
+
+    barrier = pltpu.get_barrier_semaphore()
+    greet([mid_device, core_device])
+    each(
+        groups - 1,
+        lambda k: pl.semaphore_signal(
+            barrier, inc=1, device_id=outer_device(k + 1), device_id_type=MESH_ID
+        ),
+    )
+    pl.semaphore_wait(barrier, groups + 1)
+
+    def own_copy(m):
+        return pltpu.make_async_copy(shards_in[m], wholes[m].at[index], own_sem.at[m])
+
+    def z_copy(m, k):
+        return remote(
+            shards_in[m], wholes[m].at[index], z_send.at[m, k], z_recv.at[m, k], outer_device(k)
+        )
+
+    def z_arrival(m, k):
+        origin = slot((outer - k + groups) % groups, mid, core)
+        return remote(
+            shards_in[m], wholes[m].at[origin], z_send.at[m, k], z_recv.at[m, k], outer_device(k)
+        )
+
+    def y_copy(m, k, own):
+        origin = slot((outer - k + groups) % groups, mid, core)
+        src = shards_in[m] if own else wholes[m].at[origin]
+        return remote(src, wholes[m].at[origin], y_send.at[m, k], y_recv.at[m, k], mid_device)
+
+    def y_arrival(m, k):
+        origin = slot((outer - k + groups) % groups, 1 - mid, core)
+        piece = wholes[m].at[origin]
+        return remote(piece, piece, y_send.at[m, k], y_recv.at[m, k], mid_device)
+
+    def c_copy(m, k, far, own):
+        origin = slot((outer - k + groups) % groups, 1 - mid if far else mid, core)
+        src = shards_in[m] if own else wholes[m].at[origin]
+        at = k * 2 + far
+        return remote(src, wholes[m].at[origin], c_send.at[m, at], c_recv.at[m, at], core_device)
+
+    def c_arrival(m, k, far):
+        origin = slot((outer - k + groups) % groups, 1 - mid if far else mid, 1 - core)
+        piece = wholes[m].at[origin]
+        at = k * 2 + far
+        return remote(piece, piece, c_send.at[m, at], c_recv.at[m, at], core_device)
+
+    for m in range(count):
+        each(groups - 1, lambda k: z_copy(m, k + 1).start())
+        y_copy(m, 0, True).start()
+    for m in range(count):
+        own_copy(m).start()
+        c_copy(m, 0, 0, True).start()
+    for m in range(count):
+
+        def pass_on(k):
+            z_arrival(m, k + 1).wait_recv()
+            y_copy(m, k + 1, False).start()
+            c_copy(m, k + 1, 0, False).start()
+
+        each(groups - 1, pass_on)
+    for m in range(count):
+
+        def hand_over(k):
+            y_arrival(m, k).wait_recv()
+            c_copy(m, k, 1, False).start()
+
+        each(groups, hand_over)
+    for m in range(count):
+        own_copy(m).wait()
+        each(groups - 1, lambda k: z_copy(m, k + 1).wait_send())
+
+        def finish(k):
+            y_arrival(m, k).wait_send()
+            for far in range(2):
+                c_arrival(m, k, far).wait_send()
+                c_arrival(m, k, far).wait_recv()
+
+        each(groups, finish)
+
+
+def gather_all(pieces):
+    devices = lax.axis_size("dp")
+    groups = devices // 4
+    count = len(pieces)
+    sems = [pltpu.SemaphoreType.DMA((count,))]
+    for width in (groups, groups, groups, groups, 2 * groups, 2 * groups):
+        sems.append(pltpu.SemaphoreType.DMA((count, width)))
+    return pl.pallas_call(
+        functools.partial(gather_kernel, count, groups),
+        out_shape=[jax.ShapeDtypeStruct((devices,) + p.shape, p.dtype) for p in pieces],
+        in_specs=[pl.BlockSpec(memory_space=pl.ANY)] * count,
+        out_specs=[pl.BlockSpec(memory_space=pl.ANY)] * count,
+        scratch_shapes=sems,
+        compiler_params=pltpu.CompilerParams(collective_id=1, has_side_effects=True),
+        name="gather_weights",
+    )(*pieces)
+
+
+def add_rows(target, at, other, other_at):
+    rows = target.shape[-2]
+    step = 16 if target.dtype == jnp.bfloat16 else 8
+
+    def body(r, carry):
+        where = pl.ds(r * step, step)
+        total = target[at, where, :].astype(jnp.float32) + other[other_at, where, :].astype(
+            jnp.float32
+        )
+        target[at, where, :] = total.astype(target.dtype)
+        return carry
+
+    lax.fori_loop(0, rows // step, body, 0)
+
+
+def reduce_kernel(lead_count, dec_count, groups, shapes, *refs):
+    refs = list(refs)
+
+    def grab(n):
+        taken = refs[:n]
+        del refs[:n]
+        return taken
+
+    lead_in, dec_in = grab(lead_count), grab(dec_count)
+    lead_out, dec_out = grab(lead_count), grab(dec_count)
+    lead_own, lead_c, lead_y, lead_z = (grab(lead_count) for _ in range(4))
+    dec_own, dec_c, dec_y, dec_z = (grab(dec_count) for _ in range(4))
+    load, c_send, c_recv, x_send, x_recv, y_send, y_recv, z_send, z_recv = refs
+    section, index, outer, mid, core = place()
+    x_device = (1 - section, index)
+    mid_device = (section, slot(outer, 1 - mid, core))
+    core_device = (section, slot(outer, mid, 1 - core))
+
+    def outer_device(k):
+        return (section, slot((outer + k) % groups, mid, core))
+
+    barrier = pltpu.get_barrier_semaphore()
+    greet([mid_device, core_device, x_device])
+    each(
+        groups - 1,
+        lambda k: pl.semaphore_signal(
+            barrier, inc=1, device_id=outer_device(k + 1), device_id_type=MESH_ID
+        ),
+    )
+    pl.semaphore_wait(barrier, groups + 2)
+
+    def lead_load(m, j):
+        return pltpu.make_async_copy(
+            lead_in[m].at[j * 2 + core], lead_own[m].at[j], load.at[m, j]
+        )
+
+    def lead_core(m, j):
+        return remote(
+            lead_in[m].at[j * 2 + 1 - core],
+            lead_c[m].at[j],
+            c_send.at[m, j],
+            c_recv.at[m, j],
+            core_device,
+        )
+
+    def dec_load(m, t, j):
+        at = lead_count + 2 * m + t
+        return pltpu.make_async_copy(
+            dec_in[m].at[t, j * 2 + core], dec_own[m].at[t, j], load.at[at, j]
+        )
+
+    def dec_core(m, t, j):
+        at = lead_count + 2 * m + t
+        return remote(
+            dec_in[m].at[t, j * 2 + 1 - core],
+            dec_c[m].at[t, j],
+            c_send.at[at, j],
+            c_recv.at[at, j],
+            core_device,
+        )
+
+    def x_copy(m, j):
+        return remote(
+            dec_own[m].at[0, j], dec_own[m].at[1, j], x_send.at[m, j], x_recv.at[m, j], x_device
+        )
+
+    own_of = [lead_own[m] for m in range(lead_count)] + [dec_own[m].at[1] for m in range(dec_count)]
+    y_of, z_of, out_of = lead_y + dec_y, lead_z + dec_z, lead_out + dec_out
+
+    def y_copy(n, g):
+        return remote(
+            own_of[n].at[g * 2 + 1 - mid],
+            y_of[n].at[g],
+            y_send.at[n, g],
+            y_recv.at[n, g],
+            mid_device,
+        )
+
+    def z_copy(n, k):
+        other = (outer + k) % groups
+        return remote(
+            own_of[n].at[other * 2 + mid],
+            z_of[n].at[k],
+            z_send.at[n, k],
+            z_recv.at[n, k],
+            outer_device(k),
+        )
+
+    for m in range(lead_count):
+        each(2 * groups, lambda j: lead_core(m, j).start())
+        each(2 * groups, lambda j: lead_load(m, j).start())
+
+    @pl.when(section == 1)
+    def _():
+        for m in range(dec_count):
+            for t in range(2):
+                each(2 * groups, lambda j: dec_core(m, t, j).start())
+                each(2 * groups, lambda j: dec_load(m, t, j).start())
+
+    def lead_pair(m, j):
+        lead_load(m, j).wait()
+        lead_core(m, j).wait_recv()
+        add_rows(lead_own[m], j, lead_c[m], j)
+
+    for m in range(lead_count):
+
+        def far_pair(g):
+            lead_pair(m, g * 2 + 1 - mid)
+            y_copy(m, g).start()
+
+        each(groups, far_pair)
+        each(groups, lambda g: lead_pair(m, g * 2 + mid))
+
+    @pl.when(section == 1)
+    def _():
+        for t in range(2):
+            for m in range(dec_count):
+
+                def dec_pair(j):
+                    dec_load(m, t, j).wait()
+                    dec_core(m, t, j).wait_recv()
+                    add_rows(dec_own[m].at[t], j, dec_c[m].at[t], j)
+                    if t == 0:
+                        x_copy(m, j).start()
+
+                each(2 * groups, dec_pair)
+
+    def across(n):
+        def other_rows(k):
+            other = (outer + k) % groups
+            y_copy(n, other).wait_recv()
+            add_rows(own_of[n], other * 2 + mid, y_of[n], other)
+            z_copy(n, k).start()
+
+        each(groups - 1, lambda k: other_rows(k + 1))
+        y_copy(n, outer).wait_recv()
+
+    for m in range(lead_count):
+        across(m)
+    for m in range(dec_count):
+        n = lead_count + m
+
+        @pl.when(section == 0)
+        def _():
+            each(2 * groups, lambda j: x_copy(m, j).wait_recv())
+
+        each(groups, lambda g: y_copy(n, g).start())
+    for m in range(dec_count):
+        across(lead_count + m)
+
+    for n in range(lead_count + dec_count):
+        each(groups - 1, lambda k: z_copy(n, k + 1).wait_recv())
+        own, partner, others, out = own_of[n], y_of[n], z_of[n], out_of[n]
+        rows, columns = own.shape[-2], own.shape[-1]
+        stacked = out.shape[-1] != columns
+        step = rows // 2 if stacked else (16 if own.dtype == jnp.bfloat16 else 8)
+        for r in range(rows // step):
+            where = pl.ds(r * step, step)
+
+            def total_of(lanes):
+                total = own[outer * 2 + mid, where, lanes].astype(jnp.float32)
+                total = total + partner[outer, where, lanes].astype(jnp.float32)
+                return lax.fori_loop(
+                    1, groups, lambda k, acc: acc + others[k, where, lanes].astype(jnp.float32), total
+                )
+
+            if stacked:
+                for q in range(columns // 128):
+                    lanes = slice(q * 128, q * 128 + 128)
+                    out[:, (2 * q + r) * 128 : (2 * q + r + 1) * 128] = total_of(lanes)
+            else:
+                out[where, :] = total_of(slice(None))
+
+    for m in range(lead_count):
+        each(2 * groups, lambda j: lead_core(m, j).wait_send())
+
+    @pl.when(section == 1)
+    def _():
+        for m in range(dec_count):
+            for t in range(2):
+                each(2 * groups, lambda j: dec_core(m, t, j).wait_send())
+            each(2 * groups, lambda j: x_copy(m, j).wait_send())
+
+    for n in range(lead_count + dec_count):
+        each(groups, lambda g: y_copy(n, g).wait_send())
+        each(groups - 1, lambda k: z_copy(n, k + 1).wait_send())
+
+
+def reduce_all(lead, dec, dec_outs):
+    devices = lax.axis_size("dp")
+    groups = devices // 4
+    half = devices // 2
+    nl, nd = len(lead), len(dec)
+    scratch = []
+    for lead_shape in (half, half, groups, groups):
+        scratch += [pltpu.VMEM((lead_shape,) + a.shape[1:], a.dtype) for a in lead]
+    scratch += [pltpu.VMEM((2, half) + a.shape[2:], a.dtype) for a in dec]
+    scratch += [pltpu.VMEM((2, half) + a.shape[2:], a.dtype) for a in dec]
+    for _ in range(2):
+        scratch += [pltpu.VMEM((groups,) + a.shape[2:], a.dtype) for a in dec]
+    sems = [(nl + 2 * nd, half)] * 3 + [(nd, half)] * 2 + [(nl + nd, groups)] * 4
+    outs = pl.pallas_call(
+        functools.partial(reduce_kernel, nl, nd, groups, None),
+        out_shape=[jax.ShapeDtypeStruct(a.shape[1:], jnp.float32) for a in lead]
+        + [jax.ShapeDtypeStruct(s, jnp.float32) for s in dec_outs],
+        in_specs=[pl.BlockSpec(memory_space=pl.ANY)] * (nl + nd),
+        out_specs=[pl.BlockSpec(memory_space=pltpu.VMEM)] * (nl + nd),
+        scratch_shapes=scratch + [pltpu.SemaphoreType.DMA(s) for s in sems],
+        compiler_params=pltpu.CompilerParams(
+            collective_id=2, has_side_effects=True, vmem_limit_bytes=60 << 20
+        ),
+        name="reduce_grads",
+    )(*lead, *dec)
+    return list(outs[:nl]), list(outs[nl:])
+
+
+def stack_halves(grad, devices):
+    rows, columns = grad.shape
+    r = rows // (2 * devices)
+    if r % 16 == 0:
+        return grad.reshape(2, devices, r, columns)
+    view = grad.reshape(2, devices, r, columns // 256, 2, 128)
+    return view.transpose(0, 1, 4, 2, 3, 5).reshape(2, devices, 2 * r, columns // 2)
+
+def exchange(pieces):
+    devices = lax.axis_size("dp")
+    if devices % 4 == 0 and all(p.shape[0] % 16 == 0 for p in pieces):
+        return gather_all(pieces)
+    return [lax.all_gather(p, "dp", axis=0) for p in pieces]
+
+
+def as_small(parts, rows_of):
+    flat = jnp.concatenate([p.reshape(-1) for p in parts])
+    block = rows_of * 128
+    padded = -(-flat.shape[0] // block) * block
+    return jnp.pad(flat, (0, padded - flat.shape[0])).reshape(-1, 128)
+
+
+def take_flat(flat, shapes):
+    taken, offset = [], 0
+    for shape in shapes:
+        size = 1
+        for extent in shape:
+            size *= extent
+        taken.append(flat[:, offset : offset + size].reshape((-1,) + shape))
+        offset += size
+    return taken
+
+
+def spread_columns(gathered):
+    return gathered.transpose(1, 0, 2).reshape(gathered.shape[1], -1)
+
+
+def small_chunks(vectors, bias, chunks):
+    rows, columns = vectors.shape
+    cut = vectors.reshape(rows, chunks, columns // chunks).transpose(1, 0, 2).reshape(chunks, -1)
+    flat = jnp.concatenate([cut, bias.reshape(chunks, -1)], axis=1)
+    padded = -(-flat.shape[1] // 1024) * 1024
+    return jnp.pad(flat, ((0, 0), (0, padded - flat.shape[1]))).reshape(chunks, -1, 128)
+
+
+def small_pieces(chunk, rows, chunks):
+    flat = chunk.reshape(-1)
+    vectors = rows * (D // chunks)
+    bias = FF // chunks
+    return flat[:vectors].reshape(rows, D // chunks), flat[vectors : vectors + bias]
+
+
+def total_grads(lead_big, lead_small, dec_big, dec_small):
+    devices = lax.axis_size("dp")
+    on_encoder = lax.axis_index("section") == 0
+    lead_chunks = [g.reshape(devices, -1, g.shape[1]) for g in lead_big]
+    lead_chunks.append(small_chunks(*lead_small, devices))
+    dec_chunk_small = small_chunks(*dec_small, 2 * devices)
+    dec_shapes = [(g.shape[0] // (2 * devices), g.shape[1]) for g in dec_big]
+    if devices % 4 == 0 and lead_chunks[0].shape[1] % 16 == 0:
+        dec_chunks = [stack_halves(g, devices) for g in dec_big]
+        dec_chunks.append(dec_chunk_small.reshape((2, devices) + dec_chunk_small.shape[1:]))
+        lead_out, dec_out = reduce_all(
+            lead_chunks, dec_chunks, dec_shapes + [dec_chunk_small.shape[1:]]
+        )
+    else:
+        dec_chunks = [g.reshape(2, devices, -1, g.shape[1]) for g in dec_big]
+        dec_chunks.append(dec_chunk_small.reshape((2, devices) + dec_chunk_small.shape[1:]))
+        lead_out = [
+            lax.psum_scatter(g.astype(jnp.float32), "dp", scatter_dimension=0) for g in lead_chunks
+        ]
+        dec_out = []
+        for g in dec_chunks:
+            mine = jnp.where(on_encoder, jnp.zeros_like(g), g).astype(jnp.float32)
+            mine = lax.psum_scatter(mine, "dp", scatter_dimension=1)
+            dec_out.append(lax.psum_scatter(mine, "section", scatter_dimension=0))
+    lead_vectors, lead_bias = small_pieces(lead_out[4], 12, devices)
+    dec_vectors, dec_bias = small_pieces(dec_out[4], 13, 2 * devices)
+    return lead_out[:4] + [lead_vectors, lead_bias], dec_out[:4] + [dec_vectors, dec_bias]
 
 
 def shards(
@@ -353,167 +772,65 @@
 ):
     section_id = lax.axis_index("section")
     on_encoder = section_id == 0
-    count = lax.axis_size("dp")
-    fetched = (
-        lax.all_gather(lead_qkv, "dp", axis=1, tiled=True),
-        lax.all_gather(lead_proj, "dp", axis=1, tiled=True),
-        lax.all_gather(lead_up, "dp", axis=1, tiled=True),
-        lax.all_gather(lead_down, "dp", axis=1, tiled=True),
-        lax.all_gather(lead_vectors, "dp", axis=2, tiled=True),
-        lax.all_gather(lead_bias, "dp", axis=1, tiled=True),
-        lax.all_gather(side_qkv, "dp", axis=1, tiled=True),
-        lax.all_gather(side_proj, "dp", axis=1, tiled=True),
-        lax.all_gather(side_up, "dp", axis=1, tiled=True),
-        lax.all_gather(side_down, "dp", axis=1, tiled=True),
-        lax.all_gather(side_vectors, "dp", axis=2, tiled=True),
-        lax.all_gather(side_bias, "dp", axis=1, tiled=True),
-    )
-    lead_set = (
-        fetched[0][0],
-        fetched[1][0],
-        fetched[2][0],
-        fetched[3][0],
-        fetched[4][0].astype(jnp.float32),
-        fetched[5][0].astype(jnp.float32),
-    )
-    side_set = (
-        fetched[6][0],
-        fetched[7][0],
-        fetched[8][0],
-        fetched[9][0],
-        fetched[10][0].astype(jnp.float32),
-        fetched[11][0].astype(jnp.float32),
-    )
-    crops_part = patches.shape[0] // MICRO
+    small = as_small([lead_vectors[0], lead_bias[0], side_vectors[0], side_bias[0]], 16)
+    pieces = [lead_qkv[0], lead_proj[0], lead_up[0], lead_down[0]]
+    pieces += [side_qkv[0], side_proj[0], side_up[0], side_down[0], small]
+    wholes = exchange(pieces)
+    big = [w.reshape(-1, w.shape[2]) for w in wholes[:8]]
+    flat = wholes[8].reshape(wholes[8].shape[0], -1).astype(jnp.float32)
+    lv, lb, sv, sb = take_flat(
+        flat,
+        [lead_vectors.shape[1:], lead_bias.shape[1:], side_vectors.shape[1:], side_bias.shape[1:]],
+    )
+    lead_set = tuple(big[:4]) + (spread_columns(lv), lb.reshape(-1))
+    side_set = tuple(big[4:]) + (spread_columns(sv), sb.reshape(-1))
+    crops = patches.shape[0]
     visible_count = PATCHES - MASKED
-    rows_out = [jnp.zeros((crops_part, PATCHES, D), jnp.float32) for micro_id in range(MICRO)]
-    arrived = [None] * MICRO
-    returned = [None] * MICRO
-    enc_pairs = [None] * MICRO
-    enc_small = [None] * MICRO
-    reg_pairs = [None] * MICRO
-    reg_small = [None] * MICRO
-    dec_pairs = [None] * MICRO
-    dec_small = [None] * MICRO
-    for phase_id in range(MICRO + 2):
-        if phase_id < MICRO:
-            lower = phase_id * crops_part
-            latent_pack = lax.cond(
-                on_encoder,
-                lambda: encode(
-                    patches[lower : lower + crops_part],
-                    ordering[lower : lower + crops_part],
-                    lead_set,
-                    side_set,
-                ),
-                lambda: jnp.zeros((2, crops_part, MASKED, D), jnp.bfloat16),
-            )
-        if phase_id >= 2:
-            finished = phase_id - 2
-            lower_done = finished * crops_part
-            enc_pairs[finished], enc_small[finished], rows_out[finished] = lax.cond(
-                on_encoder,
-                lambda: encode_back(
-                    patches[lower_done : lower_done + crops_part],
-                    ordering[lower_done : lower_done + crops_part],
-                    returned[finished],
-                    lead_set,
-                ),
-                lambda: (
-                    empty_pairs(crops_part, visible_count, visible_count, False),
-                    empty_small(12),
-                    rows_out[finished],
-                ),
-            )
-        if 1 <= phase_id <= MICRO:
-            current = phase_id - 1
-            lower_now = current * crops_part
-            (
-                grad_pack,
-                rows_out[current],
-                reg_pairs[current],
-                reg_small[current],
-                dec_pairs[current],
-                dec_small[current],
-            ) = lax.cond(
-                on_encoder,
-                lambda: (
-                    jnp.zeros((crops_part, visible_count, D), jnp.bfloat16),
-                    rows_out[current],
-                    empty_pairs(crops_part, MASKED, PATCHES, True),
-                    empty_small(12),
-                    empty_pairs(crops_part, MASKED, MASKED, False),
-                    empty_small(13),
-                ),
-                lambda: regress(
-                    arrived[current],
-                    ordering[lower_now : lower_now + crops_part],
-                    cotangent[lower_now : lower_now + crops_part],
-                    lead_set,
-                    side_set,
-                ),
-            )
-        if phase_id < MICRO:
-            arrived[phase_id] = passed_along(latent_pack, "section", 1)
-        if 1 <= phase_id <= MICRO:
-            returned[current] = passed_along(grad_pack, "section", -1)
-    enc_all = join_micro(enc_pairs)
-    reg_all = join_micro(reg_pairs)
-    dec_all = join_micro(dec_pairs)
+    latent_pack = lax.cond(
+        on_encoder,
+        lambda: encode(patches, ordering, lead_set, side_set),
+        lambda: jnp.zeros((2, crops, MASKED, D), jnp.bfloat16),
+    )
+    arrived = passed_along(latent_pack, "section", 1)
+    grad_pack, latent_rows, reg_pairs, reg_small, dec_pairs, dec_small = lax.cond(
+        on_encoder,
+        lambda: (
+            jnp.zeros((crops, visible_count, D), jnp.bfloat16),
+            jnp.zeros((crops, PATCHES, D), jnp.float32),
+            empty_pairs(crops, MASKED, PATCHES, True),
+            empty_small(12),
+            empty_pairs(crops, MASKED, MASKED, False),
+            empty_small(13),
+        ),
+        lambda: regress(arrived, ordering, cotangent, lead_set, side_set),
+    )
+    returned = passed_along(grad_pack, "section", -1)
+    enc_pairs, enc_small, grad_rows = lax.cond(
+        on_encoder,
+        lambda: encode_back(patches, ordering, returned, lead_set),
+        lambda: (
+            empty_pairs(crops, visible_count, visible_count, False),
+            empty_small(12),
+            latent_rows,
+        ),
+    )
+
+    def low_all(grads):
+        return tuple(g.astype(jnp.bfloat16) for g in grads)
+
     lead_big = lax.cond(
-        on_encoder, lambda: weight_grads(enc_all, False), lambda: weight_grads(reg_all, True)
-    )
-    lead_small = add_micro(enc_small + reg_small)
-    side_big = lax.cond(
         on_encoder,
-        lambda: tuple((jnp.zeros(member.shape, jnp.float32) for member in side_set[:4])),
-        lambda: weight_grads(dec_all, False),
-    )
-    side_small_sum = add_micro(dec_small)
-    grads_lead = lead_big + lead_small
-    grads_side = side_big + side_small_sum
-    column_kinds = (False, False, False, False, True, False)
-    lead_views = [lead_view(member, count, kind) for member, kind in zip(grads_lead, column_kinds)]
-    side_views = [side_view(member, count, kind) for member, kind in zip(grads_side, column_kinds)]
-    lead_widths = [view.shape[1] for view in lead_views]
-    side_widths = [view.shape[2] for view in side_views]
-    lead_total = sum(lead_widths)
-    side_total = sum(side_widths)
-    packed, width = pack_rows(
-        lead_views + [view[0] for view in side_views] + [view[1] for view in side_views], count
-    )
-    reduced = lax.psum_scatter(packed, "dp", scatter_dimension=0, tiled=True).reshape(-1)[:width]
-    lead_flat = reduced[:lead_total]
-    first_flat = reduced[lead_total : lead_total + side_total]
-    second_flat = reduced[lead_total + side_total :]
-    received = passed_along(first_flat.astype(jnp.bfloat16), "section", -1).astype(first_flat.dtype)
-    side_flat = jnp.where(on_encoder, received, second_flat)
-    lead_pieces = split_flat(lead_flat, lead_widths)
-    side_pieces = split_flat(side_flat, side_widths)
-    lead_out = [
-        lead_unview(piece, member.shape, count, kind)
-        for piece, member, kind in zip(lead_pieces, grads_lead, column_kinds)
-    ]
-    side_out = [
-        lead_unview(piece, member.shape, 2 * count, kind)
-        for piece, member, kind in zip(side_pieces, grads_side, column_kinds)
-    ]
-    section_rows = jnp.concatenate(rows_out, axis=0)[None]
-    return (
-        section_rows,
-        lead_out[0][None],
-        lead_out[1][None],
-        lead_out[2][None],
-        lead_out[3][None],
-        lead_out[4][None],
-        lead_out[5][None],
-        side_out[0],
-        side_out[1],
-        side_out[2],
-        side_out[3],
-        side_out[4],
-        side_out[5],
-    )
+        lambda: low_all(weight_grads(enc_pairs, False)),
+        lambda: low_all(weight_grads(reg_pairs, True)),
+    )
+    dec_big = lax.cond(
+        on_encoder,
+        lambda: tuple(jnp.zeros(member.shape, jnp.bfloat16) for member in side_set[:4]),
+        lambda: low_all(weight_grads(dec_pairs, False)),
+    )
+    lead_small = jax.tree.map(lambda a, b: jnp.where(on_encoder, a, b), enc_small, reg_small)
+    lead_out, dec_out = total_grads(lead_big, lead_small, dec_big, dec_small)
+    return (grad_rows[None],) + tuple(o[None] for o in lead_out) + tuple(dec_out)
 
 
 def solution(mesh):

time: 2080 us -> 714 us (0.34)
  waiting for transfers between devices: 1260 us -> 80.2 us
  Pallas kernels: 0 us -> 338 us
  local copies, waits for them, and re-layouts: 423 us -> 139 us
  blocking collectives: 100 us -> 0 us
  other arithmetic: 84.1 us -> 30 us
  loops' own time: 58 us -> 17.9 us
  matrix products: 123 us -> 99 us
    unnamed x10 -> x0, waiting for transfers between devices: 928 us -> none
    pallas_call x0 -> x2, Pallas kernels: none -> 338 us  [the longest x1 183 us: gather_all(): pl.pallas_call(functools.partial(gather_kernel, count, groups), out_shape...]
    all_gather x8 -> x0, waiting for transfers between devices: 286 us -> none  [the longest x1 54.6 us: shards(): lax.all_gather(lead_up, 'dp', axis=1, tiled=True)]
    unnamed x211 -> x43, local copies, waits for them, and re-layouts: 92.6 us -> 11.8 us
    unnamed x1 -> x0, blocking collectives: 53.1 us -> none
    reshape x14 -> x22, local copies, waits for them, and re-layouts: 111 us -> 60.8 us  [the longest x6 37.7 us: stack_halves(): view = grad.reshape(2, devices, r, columns // 256, 2, 128)]
    all_gather x2 -> x0, blocking collectives: 47 us -> none  [the longest x1 23.7 us: shards(): lax.all_gather(side_vectors, 'dp', axis=2, tiled=True)]
    another operation x8 -> x5, loops' own time: 58 us -> 17.9 us  [the longest x1 8.36 us: shards(): lax.cond(on_encoder, lambda: encode_back(patches, ordering, returned, lea...]
  transfers between devices with their start and end apart: 14 -> 2, of which waited for: 8 -> 1; matrix products, arithmetic and copies ran while one was open for 16% -> 11% of each run, Pallas kernels for 0% -> 0%
where the time goes in v1:
time: 714 us; the launch traced here: 708 us
  Pallas kernels  338 us (47%)
  local copies, waits for them, and re-layouts  139 us (19%)
  matrix products  99 us (14%)
  waiting for transfers between devices  80.2 us (11%)
  other arithmetic  30 us (4%)
  loops' own time  17.9 us (3%)
    pallas_call x1, Pallas kernels, gather_all(): pl.pallas_call(functools.partial(gather_kernel, count, groups), out_shape...  183 us
    pallas_call x1, Pallas kernels, reduce_all(): pl.pallas_call(functools.partial(reduce_kernel, nl, nd, groups, None), ou...  155 us
    ppermute x2, waiting for transfers between devices, passed_along(): return lax.ppermute(array, axis, pairs)  80.2 us
    reshape x6, local copies, waits for them, and re-layouts, stack_halves(): view = grad.reshape(2, devices, r, columns // 256, 2, 128)  37.7 us
    dot_general x9, matrix products, project(): return jnp.dot(values, weight, preferred_element_type=jnp.float32)  29.6 us
    dot_general x9, matrix products, contract_rows(): jnp.einsum('gli,glo->io', left, right, preferred_element_type=jnp.float32)  28.2 us
    dot_general x9, matrix products, back_project(): jnp.einsum('glo,io->gli', grad_rows, weight, preferred_element_type=jnp.f...  24.1 us
    reshape x3, local copies, waits for them, and re-layouts, stack_halves(): view.transpose(0, 1, 4, 2, 3, 5).reshape(2, devices, 2 * r, columns // 2)  20.2 us
  transfers between devices with their start and end apart: 2, of which 1 were waited for; matrix products, arithmetic and copies ran while one was open for 11% of the time, Pallas kernels for 0%

profile of v1, /device:TPU:3, one launch (start us, length us, event | category | flops | bytes accessed | tf_op | source)
XLA Modules:
  0.0 707.9 jit_solution(1422773612874862379)
XLA Ops:
  4.4 183.1 %gather_weights.1 = (bf16[16,48,2304]{2,1,0:T(8,128)(2,1)}, bf16[16,48,768]{2,1,0:T(8,128)(2,1)S(1)}, bf16[16,48,3072]{2,1,0:T(8,128)(2,1)}, bf16[16,192,768]{2,...) custom-call(bf16[48,2304]{1,0:T(8,128)(2,1)} %bitcast.563, ...), custom_call_target="tpu_custom_call" | custom-call | tf_op jit(solution)/shard_map/gather_weights/pallas_call | solution.py:433
  189.1 7.9 %conditional.5 = (bf16[2,2,98,768]{3,2,1,0:T(8,128)(2,1)}) conditional(s32[]{:T(128)} %convert_element_type.463, () %tuple.64, (s32[2,196]{1,0:T(2,128)S(1)}, bf16[2,196,768]{2,0,1:T(2,128)(2,1)S(1)}, f32[12,768]{1,0:T(8,128)S(1)}, bf16[768,2304]{1,0:T(8,128)(2,1)}, bf16[768,768]{1,0:T(8,128)(2,1)S(1)}, /*index=5*/bf16[768,3072]{1,0:T(8,128)(2,1)}, ...), branch_computations={%region_0.1_spmd, %region_1.19_spmd} | conditional | flops 5783490560 | bytes 119435744 | solution.py:789
  199.8 80.2 %collective-permute-done = bf16[2,2,98,768]{3,1,2,0:T(2,128)(2,1)S(1)} collective-permute-done((bf16[2,2,98,768]{3,1,2,0:T(2,128)(2,1)S(1)}, bf16[2,2,98,768]{3,1,2,0:T(2,128)(2,1)S(1)}, u32[]{:S(2)}, u32[]{:S(2)}) %collective-permute-start) | collective-permute-done | bytes 602144 | tf_op jit(solution)/shard_map/ppermute | solution.py:22
  280.1 148.3 %conditional.6 = (bf16[2,98,768]{2,1,0:T(8,128)(2,1)}, bf16[2,98,768]{2,1,0:T(8,128)(2,1)}, bf16[2,98,768]{1,2,0:T(8,128)(2,1)S(1)}, bf16[2,196,768]{2,1,0:T(8,1...) conditional(s32[]{:T(128)} %convert_element_type.463, ...), branch_computations={%region_18.79_spmd, %region_77.80_spmd} | conditional | flops 12720998400 | bytes 487558304 | solution.py:795
  310.2 8.1 %multiply_convert_fusion.1 = (bf16[2,98,3072]{2,1,0:T(8,128)(2,1)S(1)}, f32[2,98,3072]{2,1,0:T(8,128)}, f32[2,98,3072]{2,1,0:T(8,128)}) fusion(f32[3072]{0:T(1024)S(1)} %copy-done.153, bf16[2,98,768]{2,1,0:T(8,128)(2,1)S(1)} %add_convert_fusion.5, bf16[768,3072]{1,0:T(8,128)(2,1)S(1)} %bitcast.578), kind=kOutput, calls=%fused_computation.63 | convolution fusion | flops 964583424 | bytes 11053056 | tf_op jit(solution)/shard_map/cond/branch_0_fun/dot_general | solution.py:49
  338.1 8.2 %multiply_convert_fusion = (bf16[2,98,3072]{2,1,0:T(8,128)(2,1)S(1)}, f32[2,98,3072]{2,1,0:T(8,128)S(1)}, f32[2,98,3072]{2,1,0:T(8,128)S(1)}) fusion(f32[3072]{0:T(1024)S(1)} %copy-done.152, bf16[2,98,768]{2,1,0:T(8,128)(2,1)} %add_convert_fusion.3, bf16[768,3072]{1,0:T(8,128)(2,1)} %get-tuple-element.166), kind=kOutput, calls=%fused_computation.50 | convolution fusion | flops 964583424 | bytes 11053056 | tf_op jit(solution)/shard_map/cond/branch_0_fun/dot_general | solution.py:49
  350.7 4.1 convert_reduce_fusion
  355.4 3.8 fusion.419
  386.7 3.9 fusion.420
  432.2 16.3 %conditional.9 = (bf16[768,2304]{1,0:T(8,128)(2,1)}, bf16[768,768]{1,0:T(8,128)(2,1)}, bf16[768,3072]{1,0:T(8,128)(2,1)}, bf16[2,16,96,768]{3,2,1,0:T(8,128)(2,1)}) conditional(s32[]{:T(128)} %convert_element_type.463, (bf16[2,98,768]{2,1,0:T(8,128)(2,1)}, bf16[2,98,2304]{2,1,0:T(8,128)(2,1)}, bf16[2,98,768]{1,2,0:T(8,128)(2,1)}, ...), branch_computations={%region_111.114_spmd, %region_112.115_spmd} | conditional | flops 2781609984 | bytes 27402328 | solution.py:826
  434.9 4.6 bitcast_convert_fusion.9
  439.5 3.9 bitcast_convert_fusion.11
  443.4 4.9 bitcast_convert_fusion.10
  448.5 7.6 %reshape.783 = bf16[2,16,24,9,2,128]{5,4,3,2,1,0:T(2,128)(2,1)} reshape(bf16[768,2304]{1,0:T(8,128)(2,1)} %get-tuple-element.326) | data formatting | bytes 7077888 | tf_op jit(solution)/shard_map/reshape | solution.py:680
  463.9 6.2 copy.325
  470.2 8.3 %reshape.784.refs_5_ = bf16[2,16,48,1152]{3,2,1,0:T(8,128)(2,1)} reshape(bf16[2,16,2,24,9,128]{5,4,3,2,1,0:T(8,128)(2,1)} %bitcast.480) | data formatting | bytes 7077888 | tf_op jit(solution)/shard_map/reshape | solution.py:681
  478.5 11.6 %reshape.787 = bf16[2,16,24,12,2,128]{5,4,3,2,1,0:T(2,128)(2,1)} reshape(bf16[768,3072]{1,0:T(8,128)(2,1)} %get-tuple-element.328) | data formatting | bytes 9437184 | tf_op jit(solution)/shard_map/reshape | solution.py:680
  490.1 6.6 copy.324
  496.7 9.7 %reshape.788.refs_7_ = bf16[2,16,48,1536]{3,2,1,0:T(8,128)(2,1)} reshape(bf16[2,16,2,24,12,128]{5,4,3,2,1,0:T(8,128)(2,1)} %bitcast.481) | data formatting | bytes 9437184 | tf_op jit(solution)/shard_map/reshape | solution.py:681
  506.4 15.8 %conditional.7 = (bf16[2,98,768]{2,1,0:T(8,128)(2,1)S(1)}, bf16[2,98,2304]{2,1,0:T(8,128)(2,1)}, bf16[2,98,768]{1,2,0:T(8,128)(2,1)S(1)}, bf16[2,98,768]{2,1,0:T...) conditional(s32[]{:T(128)} %convert_element_type.463, ...), branch_computations={%region_78.81_spmd, %region_79.111_spmd} | conditional | flops 5803975680 | bytes 138194272 | solution.py:808
  524.2 14.1 %conditional.8 = (bf16[16,48,2304]{2,1,0:T(8,128)(2,1)}, bf16[16,48,768]{2,1,0:T(8,128)(2,1)S(1)}, bf16[16,48,3072]{2,1,0:T(8,128)(2,1)}, bf16[16,192,768]{2,1,0:T(8,128)(2,1)}) conditional(s32[]{:T(128)} %convert_element_type.463, (bf16[2,98,768]{2,1,0:T(8,128)(2,1)}, bf16[2,98,768]{1,2,0:T(8,128)(2,1)}, bf16[2,196,768]{2,1,0:T(8,128)(2,1)}, ...), branch_computations={%region_109.112_spmd, %region_110.113_spmd} | conditional | flops 3251109888 | bytes 46522568 | solution.py:821
  531.1 3.6 bitcast_convert_fusion
  534.7 3.6 bitcast_convert_fusion.1
  538.2 155.1 %reduce_grads.1 = (f32[48,2304]{1,0:T(8,128)}, f32[48,768]{1,0:T(8,128)}, f32[48,3072]{1,0:T(8,128)}, f32[192,768]{1,0:T(8,128)}, f32[8,128]{1,0:T(8,128)}, /*in...) custom-call(bf16[16,48,2304]{2,1,0:T(8,128)(2,1)} %get-tuple-element.310.r, ...), custom_call_target="tpu_custom_call" | custom-call | tf_op jit(solution)/shard_map/reduce_grads/pallas_call | solution.py:660
  (552 shorter events, 171.4 us)
Async XLA Ops:
  0.6 188.4 %copy-start.100 = (s32[2,196]{1,0:T(2,128)S(1)}, s32[2,196]{1,0:T(2,128)}, u32[]{:S(2)}) copy-start(s32[2,196]{1,0:T(2,128)} %param.31) | copy-start | bytes 4708
  0.7 188.4 %copy-start = (bf16[2,196,768]{2,0,1:T(2,128)(2,1)S(1)}, bf16[2,196,768]{2,0,1:T(2,128)(2,1)}, u32[]{:S(2)}) copy-start(bf16[2,196,768]{2,0,1:T(2,128)(2,1)} %param.29) | copy-start | bytes 1806340
  187.5 92.6 %copy-start.13 = (bf16[16,48,768]{2,1,0:T(8,128)(2,1)}, bf16[16,48,768]{2,1,0:T(8,128)(2,1)S(1)}, u32[]{:S(2)}) copy-start(bf16[16,48,768]{2,1,0:T(8,128)(2,1)S(1)} %get-tuple-element.282) | copy-start | bytes 3538948
  188.5 91.6 %copy-start.87 = (f32[16,192]{1,0:T(8,128)}, f32[16,192]{1,0:T(8,128)S(1)}, u32[]{:S(2)}) copy-start(f32[16,192]{1,0:T(8,128)S(1)} %get-tuple-element.891) | copy-start | bytes 36868
  198.5 81.5 %collective-permute-start = (bf16[2,2,98,768]{3,1,2,0:T(2,128)(2,1)S(1)}, bf16[2,2,98,768]{3,1,2,0:T(2,128)(2,1)S(1)}, u32[]{:S(2)}, u32[]{:S(2)}) collective-permute-start(bf16[2,2,98,768]{3,1,2,0:T(2,128)(2,1)S(1)} %copy.268), channel_id=1, source_target_pairs={{0,16},{1,17},{2,18},{3,19},{4,20},{5,21},{6,22},{7,23},{8,24},{9,... | collective-permute-start | bytes 1806344 | tf_op jit(solution)/shard_map/ppermute | solution.py:22
  281.0 8.7 %copy-start.24 = (bf16[768,768]{1,0:T(8,128)(2,1)}, bf16[768,768]{1,0:T(8,128)(2,1)S(1)}, u32[]{:S(2)}) copy-start(bf16[768,768]{1,0:T(8,128)(2,1)S(1)} %get-tuple-element.165) | copy-start | bytes 3538948 | tf_op jit(solution)/shard_map/cond
  281.8 12.4 %copy-start.161 = (pred[2,98]{1,0:T(4,128)(4,1)}, pred[2,98]{1,0:T(4,128)(4,1)S(1)}, u32[]{:S(2)}) copy-start(pred[2,98]{1,0:T(4,128)(4,1)S(1)} %get-tuple-element.822) | copy-start | bytes 592 | tf_op jit(solution)/shard_map/cond
  283.5 11.4 %copy-start.91 = (f32[768]{0:T(1024)}, f32[768]{0:T(1024)S(1)}, u32[]{:S(2)}) copy-start(f32[768]{0:T(1024)S(1)} %get-tuple-element.695) | copy-start | bytes 9220 | tf_op jit(solution)/shard_map/cond
  309.3 9.0 %copy-start.19 = (f32[2,98,768]{2,1,0:T(8,128)}, f32[2,98,768]{2,1,0:T(8,128)S(1)}, u32[]{:S(2)}) copy-start(f32[2,98,768]{2,1,0:T(8,128)S(1)} %get-tuple-element.776) | copy-start | bytes 1806340 | tf_op jit(solution)/shard_map/cond
  309.3 9.0 %slice-start.2 = ((s8[4718592]{0:T(1024)(128)(4,1)}), s8[4194304]{0:T(1024)(128)(4,1)S(1)}, s32[]{:S(2)}) async-start(s8[4718592]{0:T(1024)(128)(4,1)} %bitcast.474), calls=%async_computation.2 | async-start | bytes 8388608 | tf_op jit(solution)/shard_map/cond
  309.6 8.8 %copy-start.155 = (f32[2,98]{1,0:T(2,128)}, f32[2,98]{1,0:T(2,128)S(1)}, u32[]{:S(2)}) copy-start(f32[2,98]{1,0:T(2,128)S(1)} %multiply_reduce_fusion.22) | copy-start | bytes 2356 | tf_op jit(solution)/shard_map/cond
  335.6 10.7 %slice-start.10 = ((s8[4718592]{0:T(1024)(128)(4,1)}), s8[4194304]{0:T(1024)(128)(4,1)S(1)}, s32[]{:S(2)}) async-start(s8[4718592]{0:T(1024)(128)(4,1)} %bitcast.493), calls=%async_computation.10 | async-start | bytes 8388608 | tf_op jit(solution)/shard_map/cond
  336.9 18.5 %copy-start.18 = (f32[2,98,768]{2,1,0:T(8,128)}, f32[2,98,768]{2,1,0:T(8,128)S(1)}, u32[]{:S(2)}) copy-start(f32[2,98,768]{2,1,0:T(8,128)S(1)} %get-tuple-element.767) | copy-start | bytes 1806340 | tf_op jit(solution)/shard_map/cond
  429.0 77.4 %collective-permute-start.1 = (bf16[2,98,768]{2,1,0:T(8,128)(2,1)}, bf16[2,98,768]{2,1,0:T(8,128)(2,1)S(1)}, u32[]{:S(2)}, u32[]{:S(2)}) collective-permute-start(bf16[2,98,768]{2,1,0:T(8,128)(2,1)} %get-tuple-element.290), channel_id=1, source_target_pairs={{16,0},{17,1},{18,2},{19,3},{20,4},{21,5},{22,6},{23,7},{24,8},{25... | collective-permute-start | bytes 903176 | tf_op jit(solution)/shard_map/ppermute | solution.py:22
  496.7 9.7 %copy-start.14 = (bf16[16,48,768]{2,1,0:T(8,128)(2,1)S(1)}, bf16[16,48,768]{2,1,0:T(8,128)(2,1)}, u32[]{:S(2)}) copy-start(bf16[16,48,768]{2,1,0:T(8,128)(2,1)} %copy-done.13) | copy-start | bytes 3538948
  496.7 9.7 %copy-start.42 = (f32[2,196,768]{2,1,0:T(8,128)S(1)}, f32[2,196,768]{2,1,0:T(8,128)}, u32[]{:S(2)}) copy-start(f32[2,196,768]{2,1,0:T(8,128)} %get-tuple-element.289) | copy-start | bytes 3612676
  496.7 9.7 %copy-start.88 = (f32[16,192]{1,0:T(8,128)S(1)}, f32[16,192]{1,0:T(8,128)}, u32[]{:S(2)}) copy-start(f32[16,192]{1,0:T(8,128)} %copy-done.87) | copy-start | bytes 36868
  496.7 9.7 %copy-start.101 = (s32[2,196]{1,0:T(2,128)S(1)}, s32[2,196]{1,0:T(2,128)}, u32[]{:S(2)}) copy-start(s32[2,196]{1,0:T(2,128)} %param.31) | copy-start | bytes 4708
  506.4 15.9 %copy-start.154 = (f32[3072]{0:T(1024)S(1)}, f32[3072]{0:T(1024)}, u32[]{:S(2)}) copy-start(f32[3072]{0:T(1024)} %get-tuple-element.317) | copy-start | bytes 36868
  693.3 10.7 %copy-start.84 = (f32[192,768]{1,0:T(8,128)S(1)}, f32[192,768]{1,0:T(8,128)}, u32[]{:S(2)}) copy-start(f32[192,768]{1,0:T(8,128)} %get-tuple-element.335) | copy-start | bytes 1769476
  693.3 11.5 %copy-start.89 = (f32[24,2304]{1,0:T(8,128)S(1)}, f32[24,2304]{1,0:T(8,128)}, u32[]{:S(2)}) copy-start(f32[24,2304]{1,0:T(8,128)} %get-tuple-element.998) | copy-start | bytes 663556
  693.3 12.2 %copy-start.94 = (f32[24,768]{1,0:T(8,128)S(1)}, f32[24,768]{1,0:T(8,128)}, u32[]{:S(2)}) copy-start(f32[24,768]{1,0:T(8,128)} %get-tuple-element.999) | copy-start | bytes 221188
  693.4 12.8 %copy-start.86 = (f32[24,3072]{1,0:T(8,128)S(1)}, f32[24,3072]{1,0:T(8,128)}, u32[]{:S(2)}) copy-start(f32[24,3072]{1,0:T(8,128)} %get-tuple-element.1000) | copy-start | bytes 884740
  693.4 13.5 %copy-start.85 = (f32[96,768]{1,0:T(8,128)S(1)}, f32[96,768]{1,0:T(8,128)}, u32[]{:S(2)}) copy-start(f32[96,768]{1,0:T(8,128)} %get-tuple-element.1001) | copy-start | bytes 884740
  (141 other events, 444.3 us)

commit v2 on v1

--- a/solution.py
+++ b/solution.py
@@ -4,6 +4,7 @@
 import jax.experimental.pallas as pl
 import jax.experimental.pallas.tpu as pltpu
 import jax.numpy as jnp
+import numpy as np
 from jax import lax
 from jax.sharding import PartitionSpec as P
 
@@ -22,276 +23,23 @@
     return lax.ppermute(array, axis, pairs)
 
 
-def layer_norm(values, gain, shift):
-    center = values - jnp.mean(values, axis=-1, keepdims=True)
-    spread = jnp.mean(center * center, axis=-1, keepdims=True)
-    return center * lax.rsqrt(spread + 1e-06) * gain + shift
-
-
 def positions():
-    patch_ids = jnp.arange(PATCHES)
-    height = (patch_ids // GRID).astype(jnp.float32)
-    across = (patch_ids % GRID).astype(jnp.float32)
+    ids = np.arange(PATCHES)
     quarter = D // 4
-    frequency = 1.0 / 10000.0 ** (jnp.arange(quarter).astype(jnp.float32) / quarter)
-    angle_rows = height[:, None] * frequency[None, :]
-    angle_cols = across[:, None] * frequency[None, :]
-    return jnp.concatenate(
-        [jnp.sin(angle_cols), jnp.cos(angle_cols), jnp.sin(angle_rows), jnp.cos(angle_rows)], axis=1
-    )
-
-
-def gelu_exact(values):
-    return jax.nn.gelu(values, approximate=False)
-
-
-def project(values, weight):
-    return jnp.dot(values, weight, preferred_element_type=jnp.float32)
-
-
-def contract_rows(left, right):
-    return jnp.einsum("gli,glo->io", left, right, preferred_element_type=jnp.float32)
-
-
-def back_project(grad_rows, weight):
-    return jnp.einsum("glo,io->gli", grad_rows, weight, preferred_element_type=jnp.float32)
-
-
-def row_total(values):
-    return jnp.sum(values.astype(jnp.float32), axis=(0, 1))
-
-
-def split_heads(values):
-    return values.reshape(values.shape[0], values.shape[1], HEADS, HEAD_DIM)
-
-
-def attend_forward(queries, key_rows, value_rows):
-    scores = jnp.einsum(
-        "gqhd,gkhd->ghqk",
-        split_heads(queries),
-        split_heads(key_rows),
-        preferred_element_type=jnp.float32,
-    )
-    scores = scores * HEAD_DIM ** (-0.5)
-    top_score = jnp.max(scores, axis=-1, keepdims=True)
-    powers = jnp.exp(scores - top_score)
-    total_mass = jnp.sum(powers, axis=-1, keepdims=True)
-    probs = (powers / total_mass).astype(jnp.bfloat16)
-    mixed_rows = jnp.einsum(
-        "ghqk,gkhd->gqhd", probs, split_heads(value_rows), preferred_element_type=jnp.float32
-    )
-    return (
-        mixed_rows.reshape(queries.shape[0], queries.shape[1], D),
-        top_score + jnp.log(total_mass),
-    )
-
-
-def attend_backward(queries, key_rows, value_rows, log_total, grad_mixed):
-    query_heads = split_heads(queries)
-    key_heads = split_heads(key_rows)
-    scores = jnp.einsum(
-        "gqhd,gkhd->ghqk", query_heads, key_heads, preferred_element_type=jnp.float32
-    )
-    probs = jnp.exp(scores * HEAD_DIM ** (-0.5) - log_total)
-    grad_heads = split_heads(grad_mixed)
-    grad_values = jnp.einsum(
-        "ghqk,gqhd->gkhd",
-        probs.astype(jnp.bfloat16),
-        grad_heads,
-        preferred_element_type=jnp.float32,
-    )
-    grad_probs = jnp.einsum(
-        "gqhd,gkhd->ghqk", grad_heads, split_heads(value_rows), preferred_element_type=jnp.float32
-    )
-    grad_scores = probs * (grad_probs - jnp.sum(grad_probs * probs, axis=-1, keepdims=True))
-    grad_scores = grad_scores.astype(jnp.bfloat16)
-    grad_queries = jnp.einsum(
-        "ghqk,gkhd->gqhd", grad_scores, key_heads, preferred_element_type=jnp.float32
-    ) * HEAD_DIM ** (-0.5)
-    grad_keys = jnp.einsum(
-        "ghqk,gqhd->gkhd", grad_scores, query_heads, preferred_element_type=jnp.float32
-    ) * HEAD_DIM ** (-0.5)
-    rows_q = queries.shape[1]
-    rows_k = key_rows.shape[1]
-    groups = queries.shape[0]
-    return (
-        grad_queries.reshape(groups, rows_q, D).astype(jnp.bfloat16),
-        grad_keys.reshape(groups, rows_k, D).astype(jnp.bfloat16),
-        grad_values.reshape(groups, rows_k, D).astype(jnp.bfloat16),
-    )
-
-
-def run_block(stream, context, weights):
-    qkv_weight, proj_weight, up_weight, down_weight, vectors, up_bias = weights
-    rows_q = stream.shape[1]
-    source = stream if context is None else jnp.concatenate([context, stream], axis=1)
-    normed, first_back = jax.vjp(layer_norm, source, vectors[0], vectors[1])
-    normed_low = normed.astype(jnp.bfloat16)
-    if context is None:
-        combined = project(normed_low, qkv_weight)
-        queries = combined[..., :D] + vectors[6]
-        key_rows = combined[..., D : 2 * D]
-        value_rows = combined[..., 2 * D :] + vectors[7]
-    else:
-        queries = project(normed_low[:, -rows_q:], qkv_weight[:, :D]) + vectors[6]
-        pair_rows = project(normed_low, qkv_weight[:, D:])
-        key_rows = pair_rows[..., :D]
-        value_rows = pair_rows[..., D:] + vectors[7]
-    queries = queries.astype(jnp.bfloat16)
-    key_rows = key_rows.astype(jnp.bfloat16)
-    value_rows = value_rows.astype(jnp.bfloat16)
-    mixed_rows, log_total = attend_forward(queries, key_rows, value_rows)
-    mixed_low = mixed_rows.astype(jnp.bfloat16)
-    attn_out = project(mixed_low, proj_weight) + vectors[8]
-    residual = stream + vectors[10] * attn_out
-    second, second_back = jax.vjp(layer_norm, residual, vectors[2], vectors[3])
-    second_low = second.astype(jnp.bfloat16)
-    pre_gelu = project(second_low, up_weight) + up_bias
-    hidden, gelu_back = jax.vjp(gelu_exact, pre_gelu)
-    hidden_low = hidden.astype(jnp.bfloat16)
-    branch = project(hidden_low, down_weight) + vectors[9]
-    output, final_back = jax.vjp(
-        layer_norm, residual + vectors[11] * branch, vectors[4], vectors[5]
-    )
-
-    def backward(grad_out):
-        grad_final, grad_final_gain, grad_final_shift = final_back(grad_out)
-        grad_scale_two = row_total(grad_final * branch)
-        grad_branch = (vectors[11] * grad_final).astype(jnp.bfloat16)
-        grad_hidden = back_project(grad_branch, down_weight)
-        (grad_pre,) = gelu_back(grad_hidden)
-        grad_pre = grad_pre.astype(jnp.bfloat16)
-        grad_second = back_project(grad_pre, up_weight)
-        grad_resid, grad_gain_two, grad_shift_two = second_back(grad_second)
-        grad_resid = grad_resid + grad_final
-        grad_scale_one = row_total(grad_resid * attn_out)
-        grad_attn = (vectors[10] * grad_resid).astype(jnp.bfloat16)
-        grad_mixed = back_project(grad_attn, proj_weight).astype(jnp.bfloat16)
-        grad_queries, grad_keys, grad_values = attend_backward(
-            queries, key_rows, value_rows, log_total, grad_mixed
-        )
-        tail_rows = ((mixed_low, grad_attn), (second_low, grad_pre), (hidden_low, grad_branch))
-        if context is None:
-            grad_joined = jnp.concatenate([grad_queries, grad_keys, grad_values], axis=-1)
-            grad_normed = back_project(grad_joined, qkv_weight)
-            pairs = ((normed_low, grad_joined),) + tail_rows
-        else:
-            grad_pair = jnp.concatenate([grad_keys, grad_values], axis=-1)
-            grad_normed = back_project(grad_pair, qkv_weight[:, D:])
-            grad_query_rows = back_project(grad_queries, qkv_weight[:, :D])
-            grad_normed = jnp.concatenate(
-                [grad_normed[:, :-rows_q], grad_normed[:, -rows_q:] + grad_query_rows], axis=1
-            )
-            pairs = ((normed_low[:, -rows_q:], grad_queries), (normed_low, grad_pair)) + tail_rows
-        grad_source, grad_gain_one, grad_shift_one = first_back(grad_normed)
-        grad_vectors = jnp.stack(
-            [
-                grad_gain_one,
-                grad_shift_one,
-                grad_gain_two,
-                grad_shift_two,
-                grad_final_gain,
-                grad_final_shift,
-                row_total(grad_queries),
-                row_total(grad_values),
-                row_total(grad_attn),
-                row_total(grad_branch),
-                grad_scale_one,
-                grad_scale_two,
-            ]
-        )
-        grad_bias = row_total(grad_pre)
-        if context is None:
-            grad_stream = grad_resid + grad_source
-            grad_context = None
-        else:
-            grad_stream = grad_resid + grad_source[:, -rows_q:]
-            grad_context = grad_source[:, :-rows_q]
-        return (grad_stream, grad_context, pairs, (grad_vectors, grad_bias))
-
-    return (output, backward)
-
-
-def empty_pairs(count, rows_q, rows_k, cross):
-
-    def blank(rows, width):
-        return jnp.zeros((count, rows, width), jnp.bfloat16)
-
-    if cross:
-        first = ((blank(rows_q, D), blank(rows_q, D)), (blank(rows_k, D), blank(rows_k, 2 * D)))
-    else:
-        first = ((blank(rows_q, D), blank(rows_q, 3 * D)),)
-    return first + (
-        (blank(rows_q, D), blank(rows_q, D)),
-        (blank(rows_q, D), blank(rows_q, FF)),
-        (blank(rows_q, FF), blank(rows_q, D)),
-    )
-
-
-def empty_small(row_count):
-    return (jnp.zeros((row_count, D), jnp.float32), jnp.zeros((FF,), jnp.float32))
-
-
-def weight_grads(pairs, cross):
-    if cross:
-        grad_qkv = jnp.concatenate([contract_rows(*pairs[0]), contract_rows(*pairs[1])], axis=1)
-        rest = pairs[2:]
-    else:
-        grad_qkv = contract_rows(*pairs[0])
-        rest = pairs[1:]
-    return (grad_qkv, contract_rows(*rest[0]), contract_rows(*rest[1]), contract_rows(*rest[2]))
-
-
-def encode(patch_part, order_part, lead_set, side_set):
-    visible = jnp.take_along_axis(patch_part, order_part[:, MASKED:, None], axis=1).astype(
-        jnp.float32
-    )
-    masked = jnp.take_along_axis(patch_part, order_part[:, :MASKED, None], axis=1).astype(
-        jnp.float32
-    )
-    latents, unused_back = run_block(visible, None, lead_set)
-    targets, unused_teacher = run_block(masked, None, side_set)
-    return jnp.stack([latents.astype(jnp.bfloat16), targets.astype(jnp.bfloat16)])
-
-
-def encode_back(patch_part, order_part, grad_latents, lead_set):
-    visible = jnp.take_along_axis(patch_part, order_part[:, MASKED:, None], axis=1).astype(
-        jnp.float32
-    )
-    unused_out, backward = run_block(visible, None, lead_set)
-    grad_rows, unused_context, pairs, small = backward(grad_latents.astype(jnp.float32))
-    crop_ids = lax.broadcasted_iota(jnp.int32, (patch_part.shape[0], 1), 0)
-    grad_in = (
-        jnp.zeros(patch_part.shape, jnp.float32).at[crop_ids, order_part[:, MASKED:]].set(grad_rows)
-    )
-    return (pairs, small, grad_in)
-
-
-def regress(latent_pack, order_part, cot_part, lead_set, side_set):
-    pos_table = positions()
-    pos_visible = jnp.take(pos_table, order_part[:, MASKED:], axis=0)
-    pos_masked = jnp.take(pos_table, order_part[:, :MASKED], axis=0)
-    mask_queries = side_set[4][12] + pos_masked
-    latents = latent_pack[0].astype(jnp.float32)
-    targets = latent_pack[1].astype(jnp.float32)
-    regressed, regress_back = run_block(mask_queries, latents + pos_visible, lead_set)
-    decoded, decode_back = run_block(regressed + pos_masked, None, side_set)
-    grad_decode_in, unused_context, dec_pairs, dec_small = decode_back(cot_part.astype(jnp.float32))
-    grad_queries, grad_latents, reg_pairs, reg_small = regress_back(
-        grad_decode_in + regressed - targets
-    )
-    dec_small = (
-        jnp.concatenate([dec_small[0], row_total(grad_queries)[None]], axis=0),
-        dec_small[1],
-    )
-    return (
-        grad_latents.astype(jnp.bfloat16),
-        jnp.concatenate([regressed, decoded], axis=1),
-        reg_pairs,
-        reg_small,
-        dec_pairs,
-        dec_small,
-    )
+    frequency = 10000.0 ** (-np.arange(quarter) / quarter)
+    rows = (ids // GRID)[:, None] * frequency
+    cols = (ids % GRID)[:, None] * frequency
+    return np.concatenate([np.sin(cols), np.cos(cols), np.sin(rows), np.cos(rows)], axis=1)
+
+
+def position_parts():
+    rest = positions().astype(np.float32)
+    parts = []
+    for _ in range(3):
+        part = rest.astype(jnp.bfloat16)
+        rest = rest - part.astype(np.float32)
+        parts.append(part)
+    return jnp.asarray(np.stack(parts))
 
 
 MESH_ID = pl.DeviceIdType.MESH
@@ -672,17 +420,714 @@
     return list(outs[:nl]), list(outs[nl:])
 
 
-def stack_halves(grad, devices):
-    rows, columns = grad.shape
-    r = rows // (2 * devices)
-    if r % 16 == 0:
-        return grad.reshape(2, devices, r, columns)
-    view = grad.reshape(2, devices, r, columns // 256, 2, 128)
-    return view.transpose(0, 1, 4, 2, 3, 5).reshape(2, devices, 2 * r, columns // 2)
-
-def exchange(pieces):
-    devices = lax.axis_size("dp")
-    if devices % 4 == 0 and all(p.shape[0] % 16 == 0 for p in pieces):
+ROWS = 112
+LOW = jnp.bfloat16
+HIGH = jnp.float32
+VISIBLE = PATCHES - MASKED
+CHUNK = 32
+NAMES_SELF = ("normed", "qkv", "probs", "mixed", "attn", "x1", "r1", "x2", "r2", "second")
+NAMES_SELF += ("slope", "hidden", "branch", "x3", "r3")
+NAMES_CROSS = ("normed_c", "kv_c", "probs_c", "x1_c", "r1_c")
+NAMES_GRAD = ("dqkv", "dattn", "dpre", "dbranch")
+
+
+def save_shape(name, tokens):
+    pairs = tokens // ROWS * (HEADS // 2)
+    kinds = {
+        "qkv": ((tokens, 3 * D), LOW),
+        "kv_c": ((tokens, 2 * D), LOW),
+        "dqkv": ((tokens, 3 * D), LOW),
+        "dkv_c": ((tokens, 2 * D), LOW),
+        "probs": ((pairs, 2 * ROWS, ROWS), HIGH),
+        "probs_c": ((pairs, 2 * ROWS, ROWS), HIGH),
+        "hidden": ((tokens, FF), LOW),
+        "dpre": ((tokens, FF), LOW),
+        "slope": ((tokens, FF), HIGH),
+    }
+    if name in kinds:
+        return kinds[name]
+    if name in ("r1", "r2", "r3", "r1_c"):
+        return ((tokens, 1), HIGH)
+    if name in ("attn", "x1", "x1_c", "x2", "x3", "branch"):
+        return ((tokens, D), HIGH)
+    return ((tokens, D), LOW)
+
+
+def dot(left, right):
+    return jnp.dot(left, right, preferred_element_type=HIGH)
+
+
+def dot_nt(left, right):
+    return lax.dot_general(left, right, (((1,), (1,)), ((), ())), preferred_element_type=HIGH)
+
+
+def dot_tn(left, right):
+    return lax.dot_general(left, right, (((0,), (0,)), ((), ())), preferred_element_type=HIGH)
+
+
+def by_rows(tokens, body, init=()):
+    def step(i, carry):
+        return body(pl.ds(pl.multiple_of(i * CHUNK, CHUNK), CHUNK), carry)
+
+    return lax.fori_loop(0, tokens // CHUNK, step, init)
+
+
+def tiles(width, body, size=256, unroll=1):
+    def step(i, carry):
+        body(pl.ds(pl.multiple_of(i * size, size), size))
+        return carry
+
+    lax.fori_loop(0, width // size, step, 0, unroll=unroll)
+
+
+def fold(values):
+    return jnp.sum(values.reshape(-1, 8, values.shape[-1]), axis=0)
+
+
+def norm_forward(source, gain, shift, kept, spread, low, out=None):
+    def body(where, carry):
+        values = source[where, :]
+        center = values - jnp.mean(values, axis=-1, keepdims=True)
+        scale = lax.rsqrt(jnp.mean(center * center, axis=-1, keepdims=True) + 1e-06)
+        center = center * scale
+        if kept is not None:
+            kept[where, :] = center
+            spread[where, :] = scale
+        result = center * gain + shift
+        if low is not None:
+            low[where, :] = result.astype(LOW)
+        if out is not None:
+            out[where, :] = result
+        return carry
+
+    by_rows(source.shape[0], body)
+
+
+def norm_grad(grad, gain, center, scale):
+    weighted = grad * gain
+    first = jnp.mean(weighted, axis=-1, keepdims=True)
+    second = jnp.mean(weighted * center, axis=-1, keepdims=True)
+    return scale * (weighted - first - center * second)
+
+
+def pair_masks(rows):
+    lane = lax.broadcasted_iota(jnp.int32, (rows, 2 * HEAD_DIM), 1)
+    return lane < HEAD_DIM
+
+
+def two_heads(values):
+    low_lanes = pair_masks(values.shape[0])
+    zero = jnp.zeros_like(values)
+    return jnp.concatenate(
+        [jnp.where(low_lanes, values, zero), jnp.where(low_lanes, zero, values)], axis=0
+    )
+
+
+def one_pair(stacked):
+    half = stacked.shape[0] // 2
+    return jnp.where(pair_masks(half), stacked[:half], stacked[half:])
+
+
+def head_loop(tokens, body):
+    def step(p, carry):
+        for crop in range(tokens // ROWS):
+            rows = pl.ds(crop * ROWS, ROWS)
+            body(crop * (HEADS // 2) + p, rows, p)
+        return carry
+
+    lax.fori_loop(0, HEADS // 2, step, 0)
+
+
+def lanes_of(p, base):
+    return pl.ds(pl.multiple_of(base + p * 128, 128), 128)
+
+
+def attention(s, cross):
+    tokens = s["normed"].shape[0]
+    valid = lax.broadcasted_iota(jnp.int32, (2 * ROWS, ROWS), 1) < MASKED
+
+    def body(at, rows, p):
+        q2 = two_heads(s["qkv"][rows, lanes_of(p, 0)])
+        sources = [(s["qkv"][rows, lanes_of(p, D)], s["qkv"][rows, lanes_of(p, 2 * D)], "probs")]
+        if cross:
+            sources.append(
+                (s["kv_c"][rows, lanes_of(p, 0)], s["kv_c"][rows, lanes_of(p, D)], "probs_c")
+            )
+        scores = [
+            jnp.where(valid, dot_nt(q2, k) * HEAD_DIM ** (-0.5), -1e30) for k, _, _ in sources
+        ]
+        top = jnp.max(scores[0], axis=-1, keepdims=True)
+        if cross:
+            top = jnp.maximum(top, jnp.max(scores[1], axis=-1, keepdims=True))
+        powers = [jnp.exp(x - top) for x in scores]
+        mass = jnp.sum(powers[0], axis=-1, keepdims=True)
+        if cross:
+            mass = mass + jnp.sum(powers[1], axis=-1, keepdims=True)
+        mixed = None
+        inverse = 1.0 / mass
+        for power, (_, v, name) in zip(powers, sources):
+            probs = power * inverse
+            if name in s:
+                s[name][at] = probs
+            part = dot(probs.astype(LOW), v)
+            mixed = part if mixed is None else mixed + part
+        s["mixed"][rows, lanes_of(p, 0)] = one_pair(mixed).astype(LOW)
+
+    head_loop(tokens, body)
+
+
+def block_forward(s, stream, context, resid, weights, vectors, bias, out):
+    def row(r, where=slice(None)):
+        return vectors[r : r + 1, where]
+
+    norm_forward(stream, row(0), row(1), s.get("x1"), s.get("r1"), s["normed"])
+    if context is not None:
+        norm_forward(context, row(0), row(1), s["x1_c"], s["r1_c"], s["normed_c"])
+    w = weights.open(0)
+
+    def qkv_tile(j):
+        where = slice(j * 256, j * 256 + 256)
+        kind, local = divmod(j, 3)
+        extra = None if kind == 1 else row(6 if kind == 0 else 7, slice(local * 256, local * 256 + 256))
+        values = dot(s["normed"][...], w[:, where])
+        s["qkv"][:, where] = (values if extra is None else values + extra).astype(LOW)
+        if context is not None and kind > 0:
+            values = dot(s["normed_c"][...], w[:, where])
+            here = slice(j * 256 - D, j * 256 - D + 256)
+            s["kv_c"][:, here] = (values if extra is None else values + extra).astype(LOW)
+
+    for j in range(9):
+        qkv_tile(j)
+    weights.close(0)
+    attention(s, context is not None)
+    w = weights.open(1)
+    for j in range(3):
+        where = slice(j * 256, j * 256 + 256)
+        attn = dot(s["mixed"][...], w[:, where]) + row(8, where)
+        if "attn" in s:
+            s["attn"][:, where] = attn
+        resid[:, where] = stream[:, where] + row(10, where) * attn
+    weights.close(1)
+    norm_forward(resid, row(2), row(3), s.get("x2"), s.get("r2"), s["second"])
+    w = weights.open(2)
+
+    def up_tile(where):
+        pre = dot(s["second"][...], w[:, where]) + bias[0:1, where]
+        phi = 0.5 + 0.5 * lax.erf(pre * 0.5**0.5)
+        s["hidden"][:, where] = (pre * phi).astype(LOW)
+        if "slope" in s:
+            s["slope"][:, where] = phi + pre * jnp.exp(-0.5 * pre * pre) * 0.3989422804014327
+
+    tiles(FF, up_tile)
+    weights.close(2)
+    w = weights.open(3)
+    for j in range(3):
+        where = slice(j * 256, j * 256 + 256)
+        branch = dot(s["hidden"][...], w[:, where]) + row(9, where)
+        if "branch" in s:
+            s["branch"][:, where] = branch
+        resid[:, where] = resid[:, where] + row(11, where) * branch
+    weights.close(3)
+    norm_forward(resid, row(4), row(5), s.get("x3"), s.get("r3"), None, out)
+
+
+def attention_backward(s, grad_mixed, cross):
+    tokens = s["normed"].shape[0]
+    scale = HEAD_DIM ** (-0.5)
+
+    def body(at, rows, p):
+        q2 = two_heads(s["qkv"][rows, lanes_of(p, 0)])
+        g2 = two_heads(grad_mixed[rows, lanes_of(p, 0)])
+        sources = [("qkv", D, "dqkv", "probs")]
+        if cross:
+            sources.append(("kv_c", 0, "dkv_c", "probs_c"))
+        parts = []
+        inner = None
+        for name, base, grad_name, probs_name in sources:
+            v = s[name][rows, lanes_of(p, base + D)]
+            probs = s[probs_name][at]
+            s[grad_name][rows, lanes_of(p, base + D)] = dot_tn(probs.astype(LOW), g2).astype(LOW)
+            dprobs = dot_nt(g2, v)
+            parts.append((probs, dprobs))
+            total = jnp.sum(dprobs * probs, axis=-1, keepdims=True)
+            inner = total if inner is None else inner + total
+        dq = None
+        for (probs, dprobs), (name, base, grad_name, _) in zip(parts, sources):
+            dscores = (probs * (dprobs - inner)).astype(LOW)
+            part = dot(dscores, s[name][rows, lanes_of(p, base)])
+            dq = part if dq is None else dq + part
+            s[grad_name][rows, lanes_of(p, base)] = (dot_tn(dscores, q2) * scale).astype(LOW)
+        s["dqkv"][rows, lanes_of(p, 0)] = (one_pair(dq) * scale).astype(LOW)
+
+    head_loop(tokens, body)
+
+
+def block_backward(s, grad, temp, low_temp, weights, vectors, vec_grad, bias_grad, cross, context_grad):
+    tokens = grad.shape[0]
+    zero = jnp.zeros((8, D), HIGH)
+
+    def row(r):
+        return vectors[r : r + 1, :]
+
+    def put(r, total):
+        vec_grad[r : r + 1, :] = jnp.sum(total, axis=0, keepdims=True)
+
+    def final_rows(where, sums):
+        gain, shift, scale, offset = sums
+        g = grad[where, :]
+        center = s["x3"][where, :]
+        gf = norm_grad(g, row(4), center, s["r3"][where, :])
+        grad[where, :] = gf
+        low = (row(11) * gf).astype(LOW)
+        s["dbranch"][where, :] = low
+        return (
+            gain + fold(g * center),
+            shift + fold(g),
+            scale + fold(gf * s["branch"][where, :]),
+            offset + fold(low.astype(HIGH)),
+        )
+
+    sums = by_rows(tokens, final_rows, (zero,) * 4)
+    for r, total in zip((4, 5, 11, 9), sums):
+        put(r, total)
+    w = weights.open(3)
+
+    def down_tile(where):
+        low = (dot_nt(s["dbranch"][...], w[where, :]) * s["slope"][:, where]).astype(LOW)
+        s["dpre"][:, where] = low
+        bias_grad[0:1, where] = jnp.sum(low.astype(HIGH), axis=0, keepdims=True)
+
+    tiles(FF, down_tile)
+    weights.close(3)
+    w = weights.open(2)
+    for j in range(3):
+        where = slice(j * 256, j * 256 + 256)
+        temp[:, where] = dot_nt(s["dpre"][...], w[where, :])
+    weights.close(2)
+
+    def second_rows(where, sums):
+        gain, shift, scale, offset = sums
+        g = temp[where, :]
+        center = s["x2"][where, :]
+        gr = norm_grad(g, row(2), center, s["r2"][where, :]) + grad[where, :]
+        grad[where, :] = gr
+        low = (row(10) * gr).astype(LOW)
+        s["dattn"][where, :] = low
+        return (
+            gain + fold(g * center),
+            shift + fold(g),
+            scale + fold(gr * s["attn"][where, :]),
+            offset + fold(low.astype(HIGH)),
+        )
+
+    sums = by_rows(tokens, second_rows, (zero,) * 4)
+    for r, total in zip((2, 3, 10, 8), sums):
+        put(r, total)
+    w = weights.open(1)
+    for j in range(3):
+        where = slice(j * 256, j * 256 + 256)
+        low_temp[:, where] = dot_nt(s["dattn"][...], w[where, :]).astype(LOW)
+    weights.close(1)
+    attention_backward(s, low_temp, cross)
+    w = weights.open(0)
+    for j in range(3):
+        where = slice(j * 256, j * 256 + 256)
+        temp[:, where] = dot_nt(s["dqkv"][...], w[where, :])
+        if cross:
+            context_grad[:, where] = dot_nt(s["dkv_c"][...], w[where, D:])
+    weights.close(0)
+
+    def first_rows(where, sums):
+        gain, shift, dq, dv = sums
+        g = temp[where, :]
+        center = s["x1"][where, :]
+        grad[where, :] = grad[where, :] + norm_grad(g, row(0), center, s["r1"][where, :])
+        gain, shift = gain + fold(g * center), shift + fold(g)
+        dq = dq + fold(s["dqkv"][where, 0:D].astype(HIGH))
+        dv = dv + fold(s["dqkv"][where, 2 * D :].astype(HIGH))
+        if cross:
+            g = context_grad[where, :]
+            center = s["x1_c"][where, :]
+            context_grad[where, :] = norm_grad(g, row(0), center, s["r1_c"][where, :])
+            gain, shift = gain + fold(g * center), shift + fold(g)
+            dv = dv + fold(s["dkv_c"][where, D:].astype(HIGH))
+        return gain, shift, dq, dv
+
+    sums = by_rows(tokens, first_rows, (zero,) * 4)
+    for r, total in zip((0, 1, 6, 7), sums):
+        put(r, total)
+
+
+class Slots:
+    def __init__(self, places, sems):
+        self.places, self.sems = places, sems
+        self.queue = [[] for _ in places]
+        self.ready = [False] * len(places)
+
+    def copy(self, m, source):
+        return pltpu.make_async_copy(source, self.places[m], self.sems.at[m])
+
+    def plan(self, m, source):
+        self.queue[m].append(source)
+        if len(self.queue[m]) == 1:
+            self.copy(m, source).start()
+
+    def open(self, m):
+        if not self.ready[m]:
+            self.copy(m, self.queue[m][0]).wait()
+            self.ready[m] = True
+        return self.places[m]
+
+    def close(self, m):
+        self.queue[m].pop(0)
+        self.ready[m] = False
+        if self.queue[m]:
+            self.copy(m, self.queue[m][0]).start()
+
+
+class Held:
+    def __init__(self, slots):
+        self.slots = slots
+
+    def open(self, m):
+        return self.slots.open(m)
+
+    def close(self, m):
+        pass
+
+
+def transposed(place, source):
+    width = source.shape[1]
+    for j in range(width // 256):
+        where = slice(j * 256, j * 256 + 256)
+        place[where, :] = source[:, where].T
+
+
+def weight_grad(out, left, right, place, stacked=0, extra=None, base=0):
+    rows, columns = left.shape[1], right.shape[1]
+    transposed(place, left)
+    if extra is not None:
+        transposed(extra[2], extra[0])
+
+    def column_tile(j, with_extra):
+        where = pl.ds(pl.multiple_of(j * 256, 256), 256)
+        for i in range(rows // 384):
+            down = slice(i * 384, i * 384 + 384)
+            total = dot(place[down, :], right[:, where])
+            if with_extra:
+                there = pl.ds(pl.multiple_of(j * 256 - base, 256), 256)
+                total = total + dot(extra[2][down, :], extra[1][:, there])
+            if stacked:
+                count = 384 // stacked
+                cut = total.reshape(count, stacked, 256)
+                both = jnp.concatenate([cut[:, :, :128], cut[:, :, 128:]], axis=1)
+                here = pl.ds(pl.multiple_of(j * 128, 128), 128)
+                out[i * count : (i + 1) * count, :, here] = both.astype(LOW)
+            else:
+                out[down, where] = total.astype(LOW)
+
+    def plain(j, carry):
+        column_tile(j, False)
+        return carry
+
+    def joined(j, carry):
+        column_tile(j, True)
+        return carry
+
+    first = base // 256 if extra is not None else columns // 256
+    lax.fori_loop(0, first, plain, 0)
+    if extra is not None:
+        lax.fori_loop(first, columns // 256, joined, 0)
+
+
+def crop_rows(c):
+    return slice(c * ROWS, c * ROWS + ROWS)
+
+
+def one_hot(orders, kind, crop):
+    ids = orders[kind, crop_rows(crop), :]
+    return (ids == lax.broadcasted_iota(jnp.int32, (ROWS, PATCHES), 1)).astype(LOW)
+
+
+def encode_kernel(crops, *refs):
+    refs = list(refs)
+    patches, orders, pos = refs[:3]
+    lead_w, side_w = refs[3:7], refs[7:11]
+    lead_vec, lead_bias, side_vec, side_bias = refs[11:15]
+    pack, pos_visible, pos_masked = refs[15:18]
+    refs = refs[18:]
+    saved = dict(zip(NAMES_SELF, refs))
+    refs = refs[len(NAMES_SELF) :]
+    places, (sems, stream, resid, latent) = refs[:4], refs[4:8]
+    brief = dict(zip(("normed", "qkv", "mixed", "second", "hidden"), refs[8:13]))
+    section = lax.axis_index("section")
+
+    @pl.when(section == 0)
+    def _():
+        slots = Slots(places, sems)
+        for source in (lead_w, side_w):
+            for m in range(4):
+                slots.plan(m, source[m])
+        for kind in range(2):
+            for c in range(crops):
+                rows = dot(one_hot(orders, kind, c), patches[c])
+                stream[crop_rows(c), :] = rows
+            if kind == 0:
+                block_forward(saved, stream, None, resid, slots, lead_vec, lead_bias, latent)
+            else:
+                block_forward(brief, stream, None, resid, slots, side_vec, side_bias, latent)
+            pack[kind] = latent[...].astype(LOW)
+
+    @pl.when(section == 1)
+    def _():
+        for kind, place_of in enumerate((pos_visible, pos_masked)):
+            for c in range(crops):
+                pick = one_hot(orders, kind, c)
+                place_of[crop_rows(c), :] = sum(dot(pick, pos[t]) for t in (2, 1, 0))
+
+
+def regress_kernel(crops, *refs):
+    refs = list(refs)
+    pack, pos_visible, pos_masked, cotangent = refs[:4]
+    lead_w, side_w = refs[4:8], refs[8:12]
+    lead_vec, lead_bias, side_vec, side_bias = refs[12:16]
+    refs = refs[16:]
+
+    def grab(names):
+        taken = dict(zip(names, refs))
+        del refs[: len(names)]
+        return taken
+
+    grad_latents, rows_out, reg_vec, reg_bias, dec_vec, dec_bias = refs[:6]
+    del refs[:6]
+    reg, dec = grab(OUT_REG), grab(OUT_DEC)
+    reg.update(grab(KEEP_REG))
+    dec.update(grab(KEEP_DEC))
+    places = refs[:4]
+    sems, stream, context, resid, regressed, grad, temp, low_temp = refs[4:]
+    tokens = crops * ROWS
+
+    @pl.when(lax.axis_index("section") == 1)
+    def _():
+        slots = Slots(places, sems)
+        for source in (lead_w, side_w, lead_w):
+            for m in range(4):
+                slots.plan(m, source[m])
+        stream[...] = side_vec[12:13, :] + pos_masked[...]
+        context[...] = pack[0].astype(HIGH) + pos_visible[...]
+        block_forward(reg, stream, context, resid, slots, lead_vec, lead_bias, regressed)
+        stream[...] = regressed[...] + pos_masked[...]
+        block_forward(dec, stream, None, resid, Held(slots), side_vec, side_bias, temp)
+        for c in range(crops):
+            first = c * ROWS
+            rows_out[c, 0:MASKED, :] = regressed[first : first + MASKED, :]
+            rows_out[c, MASKED : 2 * MASKED, :] = temp[first : first + MASKED, :]
+            grad[first : first + ROWS, :] = jnp.zeros((ROWS, D), HIGH)
+            grad[first : first + MASKED, :] = cotangent[c].astype(HIGH)
+        block_backward(
+            dec, grad, temp, low_temp, slots, side_vec, dec_vec, dec_bias, False, None
+        )
+        inside = lax.broadcasted_iota(jnp.int32, (ROWS, D), 0) < MASKED
+        for c in range(crops):
+            here = crop_rows(c)
+            apart = regressed[here, :] - pack[1, here, :].astype(HIGH)
+            grad[here, :] = grad[here, :] + jnp.where(inside, apart, 0.0)
+        block_backward(
+            reg, grad, temp, low_temp, slots, lead_vec, reg_vec, reg_bias, True, context
+        )
+        dec_vec[12:13, :] = jnp.sum(grad[...], axis=0, keepdims=True)
+        grad_latents[...] = context[...].astype(LOW)
+
+
+PAIRS = (("normed", "dqkv"), ("mixed", "dattn"), ("second", "dpre"), ("hidden", "dbranch"))
+OUT_DEC = tuple(n for pair in PAIRS for n in pair)
+OUT_REG = OUT_DEC + ("normed_c", "dkv_c")
+KEEP_DEC = tuple(n for n in NAMES_SELF if n not in OUT_DEC)
+KEEP_REG = KEEP_DEC + tuple(n for n in NAMES_CROSS if n not in OUT_REG)
+
+
+def ship(m, scratch, outs, sems):
+    return pltpu.make_async_copy(scratch[m], outs[m], sems.at[m])
+
+
+def decoder_weights_kernel(stacks, *refs):
+    pairs, outs = dict(zip(OUT_DEC, refs[:8])), refs[8:12]
+    scratch, (place, sems) = refs[12:16], refs[16:]
+
+    @pl.when(lax.axis_index("section") == 1)
+    def _():
+        for m in (3, 2, 1, 0):
+            left, right = PAIRS[m]
+            rows = pairs[left].shape[1]
+            weight_grad(
+                scratch[m], pairs[left], pairs[right], place.at[0:rows, :], stacks[m]
+            )
+            ship(m, scratch, outs, sems).start()
+        for m in range(4):
+            ship(m, scratch, outs, sems).wait()
+
+
+def finish_kernel(crops, *refs):
+    refs = list(refs)
+    returned, orders = refs[:2]
+    lead_w, lead_vec, lead_bias = refs[2:6], refs[6], refs[7]
+    del refs[:8]
+
+    def grab(names):
+        taken = dict(zip(names, refs))
+        del refs[: len(names)]
+        return taken
+
+    enc, reg = grab(NAMES_SELF), grab(OUT_REG)
+    outs, (rows_out, enc_vec, enc_bias) = refs[:4], refs[4:7]
+    del refs[:7]
+    enc.update(grab(NAMES_GRAD))
+    places = refs[:4]
+    scratch = refs[4:8]
+    sems, out_sems, place, place_c, grad, temp, low_temp = refs[8:]
+    section = lax.axis_index("section")
+
+    def weights_of(pairs, joined):
+        for m in (3, 2, 1, 0):
+            left, right = PAIRS[m]
+            rows = pairs[left].shape[1]
+            extra = (pairs["normed_c"], pairs["dkv_c"], place_c) if joined and m == 0 else None
+            weight_grad(
+                scratch[m], pairs[left], pairs[right], place.at[0:rows, :], 0, extra, D
+            )
+            ship(m, scratch, outs, out_sems).start()
+        for m in range(4):
+            ship(m, scratch, outs, out_sems).wait()
+
+    @pl.when(section == 0)
+    def _():
+        slots = Slots(places, sems)
+        for m in (3, 2, 1, 0):
+            slots.plan(m, lead_w[m])
+        grad[...] = returned[...].astype(HIGH)
+        block_backward(enc, grad, temp, low_temp, slots, lead_vec, enc_vec, enc_bias, False, None)
+        for c in range(crops):
+            rest = grad[crop_rows(c), :]
+            pick = one_hot(orders, 0, c)
+            total = jnp.zeros((PATCHES, D), HIGH)
+            for _ in range(3):
+                part = rest.astype(LOW)
+                rest = rest - part.astype(HIGH)
+                total = total + dot_tn(pick, part)
+            rows_out[c] = total
+        weights_of(enc, False)
+
+    @pl.when(section == 1)
+    def _():
+        weights_of(reg, True)
+
+
+ANYWHERE = pl.BlockSpec(memory_space=pl.ANY)
+INSIDE = pl.BlockSpec(memory_space=pltpu.VMEM)
+
+
+def specs(shapes):
+    return [jax.ShapeDtypeStruct(s, d) for s, d in shapes]
+
+
+def places_for(shapes):
+    return [pltpu.VMEM(s, d) for s, d in shapes]
+
+
+def params():
+    return pltpu.CompilerParams(vmem_limit_bytes=60 << 20)
+
+
+WEIGHT_SHAPES = [((D, 3 * D), LOW), ((D, D), LOW), ((D, FF), LOW), ((FF, D), LOW)]
+SMALL_SHAPES = [((16, D), HIGH), ((1, FF), HIGH)]
+
+
+def encode(crops, patches, orders, pos, lead_w, side_w, smalls):
+    tokens = crops * ROWS
+    shapes = [((2, tokens, D), LOW), ((tokens, D), HIGH), ((tokens, D), HIGH)]
+    shapes += [save_shape(n, tokens) for n in NAMES_SELF]
+    scratch = places_for(WEIGHT_SHAPES) + [pltpu.SemaphoreType.DMA((4,))]
+    scratch += places_for([((tokens, D), HIGH)] * 3)
+    scratch += places_for(
+        [save_shape(n, tokens) for n in ("normed", "qkv", "mixed", "second", "hidden")]
+    )
+    return pl.pallas_call(
+        functools.partial(encode_kernel, crops),
+        out_shape=specs(shapes),
+        in_specs=[INSIDE] * 3 + [ANYWHERE] * 8 + [INSIDE] * 4,
+        out_specs=[INSIDE] * len(shapes),
+        scratch_shapes=scratch,
+        compiler_params=params(),
+        name="encode",
+    )(patches, orders, pos, *lead_w, *side_w, *smalls)
+
+
+def regress(crops, pack, pos_visible, pos_masked, cotangent, lead_w, side_w, smalls):
+    tokens = crops * ROWS
+    shapes = [((tokens, D), LOW), ((crops, PATCHES, D), HIGH)] + SMALL_SHAPES * 2
+    shapes += [save_shape(n, tokens) for n in OUT_REG + OUT_DEC]
+    scratch = places_for([save_shape(n, tokens) for n in KEEP_REG + KEEP_DEC])
+    scratch += places_for(WEIGHT_SHAPES) + [pltpu.SemaphoreType.DMA((4,))]
+    scratch += places_for([((tokens, D), HIGH)] * 6 + [((tokens, D), LOW)])
+    return pl.pallas_call(
+        functools.partial(regress_kernel, crops),
+        out_shape=specs(shapes),
+        in_specs=[INSIDE] * 4 + [ANYWHERE] * 8 + [INSIDE] * 4,
+        out_specs=[INSIDE] * len(shapes),
+        scratch_shapes=scratch,
+        compiler_params=params(),
+        name="regress",
+    )(pack, pos_visible, pos_masked, cotangent, *lead_w, *side_w, *smalls)
+
+
+def dec_grad_shapes(devices, own_path):
+    shapes, stacks = [], []
+    for (rows, columns), kind in WEIGHT_SHAPES:
+        r = rows // (2 * devices)
+        stack = r if own_path and r % 16 else 0
+        stacks.append(stack)
+        shapes.append(
+            ((2 * devices, 2 * r, columns // 2), kind) if stack else ((rows, columns), kind)
+        )
+    return shapes, tuple(stacks)
+
+
+def decoder_weights(crops, pairs, devices, own_path):
+    shapes, stacks = dec_grad_shapes(devices, own_path)
+    return pl.pallas_call(
+        functools.partial(decoder_weights_kernel, stacks),
+        out_shape=specs(shapes),
+        in_specs=[INSIDE] * 8,
+        out_specs=[ANYWHERE] * 4,
+        scratch_shapes=places_for(shapes)
+        + places_for([((FF, crops * ROWS), LOW)])
+        + [pltpu.SemaphoreType.DMA((4,))],
+        compiler_params=params(),
+        name="decoder_weights",
+    )(*pairs)
+
+
+def finish(crops, returned, orders, lead_w, lead_small, enc_saved, reg_pairs):
+    tokens = crops * ROWS
+    shapes = WEIGHT_SHAPES + [((crops, PATCHES, D), HIGH)] + SMALL_SHAPES
+    scratch = places_for([save_shape(n, tokens) for n in NAMES_GRAD])
+    scratch += places_for(WEIGHT_SHAPES * 2) + [pltpu.SemaphoreType.DMA((4,))] * 2
+    scratch += places_for([((FF, tokens), LOW), ((D, tokens), LOW)])
+    scratch += places_for([((tokens, D), HIGH)] * 2 + [((tokens, D), LOW)])
+    count = len(enc_saved) + len(reg_pairs)
+    return pl.pallas_call(
+        functools.partial(finish_kernel, crops),
+        out_shape=specs(shapes),
+        in_specs=[INSIDE] * 2 + [ANYWHERE] * 4 + [INSIDE] * (2 + count),
+        out_specs=[ANYWHERE] * 4 + [INSIDE] * 3,
+        scratch_shapes=scratch,
+        compiler_params=params(),
+        name="finish",
+    )(returned, orders, *lead_w, *lead_small, *enc_saved, *reg_pairs)
+
+
+def exchange(pieces, own_path):
+    if own_path:
         return gather_all(pieces)
     return [lax.all_gather(p, "dp", axis=0) for p in pieces]
 
@@ -724,15 +1169,20 @@
     return flat[:vectors].reshape(rows, D // chunks), flat[vectors : vectors + bias]
 
 
-def total_grads(lead_big, lead_small, dec_big, dec_small):
+def total_grads(lead_big, lead_small, dec_big, dec_small, own_path):
     devices = lax.axis_size("dp")
     on_encoder = lax.axis_index("section") == 0
+    dec_shapes = [(rows // (2 * devices), columns) for (rows, columns), _ in WEIGHT_SHAPES]
     lead_chunks = [g.reshape(devices, -1, g.shape[1]) for g in lead_big]
     lead_chunks.append(small_chunks(*lead_small, devices))
     dec_chunk_small = small_chunks(*dec_small, 2 * devices)
-    dec_shapes = [(g.shape[0] // (2 * devices), g.shape[1]) for g in dec_big]
-    if devices % 4 == 0 and lead_chunks[0].shape[1] % 16 == 0:
-        dec_chunks = [stack_halves(g, devices) for g in dec_big]
+    if own_path:
+        dec_chunks = [
+            g.reshape(2, devices, *g.shape[1:])
+            if g.ndim == 3
+            else g.reshape(2, devices, -1, g.shape[1])
+            for g in dec_big
+        ]
         dec_chunks.append(dec_chunk_small.reshape((2, devices) + dec_chunk_small.shape[1:]))
         lead_out, dec_out = reduce_all(
             lead_chunks, dec_chunks, dec_shapes + [dec_chunk_small.shape[1:]]
@@ -751,6 +1201,12 @@
     lead_vectors, lead_bias = small_pieces(lead_out[4], 12, devices)
     dec_vectors, dec_bias = small_pieces(dec_out[4], 13, 2 * devices)
     return lead_out[:4] + [lead_vectors, lead_bias], dec_out[:4] + [dec_vectors, dec_bias]
+
+
+def padded_orders(ordering, part):
+    cut = ordering[:, MASKED:] if part == 0 else ordering[:, :MASKED]
+    cut = jnp.pad(cut, ((0, 0), (0, ROWS - MASKED)), constant_values=-1)
+    return cut.reshape(-1, 1)
 
 
 def shards(
@@ -770,67 +1226,49 @@
     side_vectors,
     side_bias,
 ):
-    section_id = lax.axis_index("section")
-    on_encoder = section_id == 0
+    on_encoder = lax.axis_index("section") == 0
+    devices = lax.axis_size("dp")
+    own_path = devices % 4 == 0 and lead_qkv.shape[1] % 16 == 0
+    crops = patches.shape[0]
     small = as_small([lead_vectors[0], lead_bias[0], side_vectors[0], side_bias[0]], 16)
     pieces = [lead_qkv[0], lead_proj[0], lead_up[0], lead_down[0]]
     pieces += [side_qkv[0], side_proj[0], side_up[0], side_down[0], small]
-    wholes = exchange(pieces)
+    wholes = exchange(pieces, own_path)
     big = [w.reshape(-1, w.shape[2]) for w in wholes[:8]]
-    flat = wholes[8].reshape(wholes[8].shape[0], -1).astype(jnp.float32)
+    flat = wholes[8].reshape(devices, -1).astype(jnp.float32)
     lv, lb, sv, sb = take_flat(
         flat,
         [lead_vectors.shape[1:], lead_bias.shape[1:], side_vectors.shape[1:], side_bias.shape[1:]],
     )
-    lead_set = tuple(big[:4]) + (spread_columns(lv), lb.reshape(-1))
-    side_set = tuple(big[4:]) + (spread_columns(sv), sb.reshape(-1))
-    crops = patches.shape[0]
-    visible_count = PATCHES - MASKED
-    latent_pack = lax.cond(
-        on_encoder,
-        lambda: encode(patches, ordering, lead_set, side_set),
-        lambda: jnp.zeros((2, crops, MASKED, D), jnp.bfloat16),
+
+    def sixteen(vectors):
+        rows = spread_columns(vectors)
+        return jnp.pad(rows, ((0, 16 - rows.shape[0]), (0, 0)))
+
+    lead_w, side_w = big[:4], big[4:]
+    lead_small = [sixteen(lv), lb.reshape(1, -1)]
+    smalls = lead_small + [sixteen(sv), sb.reshape(1, -1)]
+    orders = jnp.stack([padded_orders(ordering, 0), padded_orders(ordering, 1)])
+    pack, pos_visible, pos_masked, *enc_saved = encode(
+        crops, patches, orders, position_parts(), lead_w, side_w, smalls
     )
-    arrived = passed_along(latent_pack, "section", 1)
-    grad_pack, latent_rows, reg_pairs, reg_small, dec_pairs, dec_small = lax.cond(
-        on_encoder,
-        lambda: (
-            jnp.zeros((crops, visible_count, D), jnp.bfloat16),
-            jnp.zeros((crops, PATCHES, D), jnp.float32),
-            empty_pairs(crops, MASKED, PATCHES, True),
-            empty_small(12),
-            empty_pairs(crops, MASKED, MASKED, False),
-            empty_small(13),
-        ),
-        lambda: regress(arrived, ordering, cotangent, lead_set, side_set),
+    arrived = passed_along(pack, "section", 1)
+    grad_latents, latent_rows, reg_vec, reg_bias, dec_vec, dec_bias, *pairs = regress(
+        crops, arrived, pos_visible, pos_masked, cotangent, lead_w, side_w, smalls
     )
-    returned = passed_along(grad_pack, "section", -1)
-    enc_pairs, enc_small, grad_rows = lax.cond(
-        on_encoder,
-        lambda: encode_back(patches, ordering, returned, lead_set),
-        lambda: (
-            empty_pairs(crops, visible_count, visible_count, False),
-            empty_small(12),
-            latent_rows,
-        ),
+    reg_pairs, dec_pairs = pairs[: len(OUT_REG)], pairs[len(OUT_REG) :]
+    returned = passed_along(grad_latents, "section", -1)
+    dec_big = decoder_weights(crops, dec_pairs, devices, own_path)
+    *lead_big, grad_rows, enc_vec, enc_bias = finish(
+        crops, returned, orders, lead_w, lead_small, enc_saved, reg_pairs
     )
-
-    def low_all(grads):
-        return tuple(g.astype(jnp.bfloat16) for g in grads)
-
-    lead_big = lax.cond(
-        on_encoder,
-        lambda: low_all(weight_grads(enc_pairs, False)),
-        lambda: low_all(weight_grads(reg_pairs, True)),
+    vec = jnp.where(on_encoder, enc_vec, reg_vec)[:12]
+    bias = jnp.where(on_encoder, enc_bias, reg_bias)
+    lead_out, dec_out = total_grads(
+        lead_big, (vec, bias[0]), dec_big, (dec_vec[:13], dec_bias[0]), own_path
     )
-    dec_big = lax.cond(
-        on_encoder,
-        lambda: tuple(jnp.zeros(member.shape, jnp.bfloat16) for member in side_set[:4]),
-        lambda: low_all(weight_grads(dec_pairs, False)),
-    )
-    lead_small = jax.tree.map(lambda a, b: jnp.where(on_encoder, a, b), enc_small, reg_small)
-    lead_out, dec_out = total_grads(lead_big, lead_small, dec_big, dec_small)
-    return (grad_rows[None],) + tuple(o[None] for o in lead_out) + tuple(dec_out)
+    rows = jnp.where(on_encoder, grad_rows, latent_rows)
+    return (rows[None],) + tuple(o[None] for o in lead_out) + tuple(dec_out)
 
 
 def solution(mesh):

time: 714 us -> 547 us (0.77)
  Pallas kernels: 338 us -> 459 us
  local copies, waits for them, and re-layouts: 139 us -> 25.6 us
  matrix products: 99 us -> 0 us
  waiting for transfers between devices: 80.2 us -> 46.7 us
  other arithmetic: 30 us -> 3.96 us
  loops' own time: 17.9 us -> 0 us
    pallas_call x0 -> x4, Pallas kernels: none -> 112 us  [the longest x1 72.4 us: regress(): pl.pallas_call(functools.partial(regress_kernel, crops), out_shape=specs(...]
    dot_general x39 -> x0, matrix products: 99 us -> none  [the longest x9 29.6 us: project(): return jnp.dot(values, weight, preferred_element_type=jnp.float32)]
    reshape x11 -> x2, local copies, waits for them, and re-layouts: 58.6 us -> 1.36 us  [the longest x1 0.68 us: shards(): lead_small = [sixteen(lv), lb.reshape(1, -1)]]
    ppermute x2, waiting for transfers between devices: 80.2 us -> 46.7 us  [passed_along(): return lax.ppermute(array, axis, pairs)]
    another operation x37 -> x6, local copies, waits for them, and re-layouts: 21.7 us -> 1.2 us  [the longest x1 0.68 us: shards(): return (rows[None],) + tuple((o[None] for o in lead_out)) + tuple(dec_out)]
    another operation x5 -> x0, loops' own time: 17.9 us -> none  [the longest x1 8.36 us: shards(): lax.cond(on_encoder, lambda: encode_back(patches, ordering, returned, lea...]
    reduce_sum x26 -> x0, other arithmetic: 14.4 us -> none  [the longest x6 6.05 us: row_total(): return jnp.sum(values.astype(jnp.float32), axis=(0, 1))]
    convert_element_type x11 -> x0, local copies, waits for them, and re-layouts: 14.1 us -> none  [the longest x2 4.14 us: attend_backward(): grad_values.reshape(groups, rows_k, D).astype(jnp.bfloat16)]
  transfers between devices with their start and end apart: 2 -> 2, of which waited for: 1 -> 1; matrix products, arithmetic and copies ran while one was open for 11% -> 1% of each run, Pallas kernels for 0% -> 2%
where the time goes in v2:
time: 547 us; the launch traced here: 539 us
  Pallas kernels  459 us (84%)
  waiting for transfers between devices  46.7 us (9%)
  local copies, waits for them, and re-layouts  25.6 us (5%)
    pallas_call x1, Pallas kernels, gather_all(): pl.pallas_call(functools.partial(gather_kernel, count, groups), out_shape...  183 us
    pallas_call x1, Pallas kernels, reduce_all(): pl.pallas_call(functools.partial(reduce_kernel, nl, nd, groups, None), ou...  164 us
    pallas_call x1, Pallas kernels, regress(): pl.pallas_call(functools.partial(regress_kernel, crops), out_shape=specs(...  72.4 us
    ppermute x2, waiting for transfers between devices, passed_along(): return lax.ppermute(array, axis, pairs)  46.7 us
    pallas_call x1, Pallas kernels, finish(): pl.pallas_call(functools.partial(finish_kernel, crops), out_shape=specs(s...  19 us
    unnamed x55, local copies, waits for them, and re-layouts  13.6 us
    pallas_call x1, Pallas kernels, decoder_weights(): pl.pallas_call(functools.partial(decoder_weights_kernel, stacks), out_sha...  13.3 us
  transfers between devices with their start and end apart: 2, of which 1 were waited for; matrix products, arithmetic and copies ran while one was open for 1% of the time, Pallas kernels for 2%

profile of v2, /device:TPU:3, one launch (start us, length us, event | category | flops | bytes accessed | tf_op | source)
XLA Modules:
  0.0 539.2 jit_solution(11555835648089709941)
XLA Ops:
  0.7 0.8 reshape_squeeze.12
  1.5 0.8 reshape_squeeze.13
  4.4 183.1 %gather_weights.1 = (bf16[16,48,2304]{2,1,0:T(8,128)(2,1)}, bf16[16,48,768]{2,1,0:T(8,128)(2,1)}, bf16[16,48,3072]{2,1,0:T(8,128)(2,1)}, bf16[16,192,768]{2,1,0:...) custom-call(bf16[48,2304]{1,0:T(8,128)(2,1)} %bitcast.101, ...), custom_call_target="tpu_custom_call" | custom-call | tf_op jit(solution)/shard_map/gather_weights/pallas_call | solution.py:181
  187.5 0.9 copy.74
  188.4 0.9 copy.63.refs_0_
  193.7 7.2 %encode.1 = (bf16[2,224,768]{2,1,0:T(8,128)(2,1)}, f32[224,768]{1,0:T(8,128)}, f32[224,768]{1,0:T(8,128)}, bf16[224,768]{1,0:T(8,128)(2,1)}, bf16[224,2304]{1,0:...) custom-call(bf16[2,196,768]{2,1,0:T(8,128)(2,1)} %copy.63.refs_0_, ...), custom_call_target="tpu_custom_call" | custom-call | tf_op jit(solution)/shard_map/encode/pallas_call | solution.py:1054
  200.9 1.3 collective-permute-start
  202.2 0.8 copy.64.refs_3_
  202.9 46.7 %collective-permute-done.refs_0_ = bf16[2,224,768]{2,1,0:T(8,128)(2,1)S(1)} collective-permute-done((bf16[2,224,768]{2,1,0:T(8,128)(2,1)}, bf16[2,224,768]{2,1,0:T(8,128)(2,1)S(1)}, u32[]{:S(2)}, u32[]{:S(2)}) %collective-permute-start) | collective-permute-done | bytes 688160 | tf_op jit(solution)/shard_map/ppermute | solution.py:23
  249.6 0.9 copy-done.3
  250.5 72.4 %regress.1 = (bf16[224,768]{1,0:T(8,128)(2,1)}, f32[2,196,768]{2,1,0:T(8,128)}, f32[16,768]{1,0:T(8,128)}, f32[1,3072]{1,0:T(1,128)}, f32[16,768]{1,0:T(8,128)},...) custom-call(bf16[2,224,768]{2,1,0:T(8,128)(2,1)} %copy-done.3, ...), custom_call_target="tpu_custom_call" | custom-call | tf_op jit(solution)/shard_map/regress/pallas_call | solution.py:1072
  322.9 1.3 collective-permute-start.1
  324.7 1.4 reduce.9
  326.2 1.0 reshape.148
  328.1 13.3 %decoder_weights.1 = (bf16[32,48,1152]{2,1,0:T(8,128)(2,1)}, bf16[32,48,384]{2,1,0:T(8,128)(2,1)}, bf16[32,48,1536]{2,1,0:T(8,128)(2,1)}, bf16[3072,768]{1,0:T(8,128)(2,1)}) custom-call(bf16[224,768]{1,0:T(8,128)(2,1)} %get-tuple-element.133.refs_0_, bf16[224,2304]{1,0:T(8,128)(2,1)} %get-tuple-element.134.refs_1_, ...), custom_call_target="tpu_custom_call" | custom-call | tf_op jit(solution)/shard_map/decoder_weights/pallas_call | solution.py:1097
  341.4 0.7 copy-done.8
  342.2 19.0 %finish.1 = (bf16[768,2304]{1,0:T(8,128)(2,1)}, bf16[768,768]{1,0:T(8,128)(2,1)}, bf16[768,3072]{1,0:T(8,128)(2,1)}, bf16[3072,768]{1,0:T(8,128)(2,1)}, f32[2,19...) custom-call(bf16[224,768]{1,0:T(8,128)(2,1)} %copy-done.8, s32[2,224,1]{2,1,0:T(8,128)} %copy-done, ...), custom_call_target="tpu_custom_call" | custom-call | tf_op jit(solution)/shard_map/finish/pallas_call | solution.py:1118
  361.3 0.8 slice_select_fusion
  363.0 164.2 %reduce_grads.1 = (f32[48,2304]{1,0:T(8,128)}, f32[48,768]{1,0:T(8,128)}, f32[48,3072]{1,0:T(8,128)}, f32[192,768]{1,0:T(8,128)}, f32[8,128]{1,0:T(8,128)}, /*in...) custom-call(bf16[16,48,2304]{2,1,0:T(8,128)(2,1)} %bitcast.81, ...), custom_call_target="tpu_custom_call" | custom-call | tf_op jit(solution)/shard_map/reduce_grads/pallas_call | solution.py:408
  527.9 1.3 slice.48
  529.3 1.6 copy.68
  533.0 0.8 copy.85
  534.4 0.8 copy.87
  535.2 0.8 copy.88
  (86 shorter events, 15.4 us)
Async XLA Ops:
  0.6 187.8 %copy-start.4 = (bf16[2,196,768]{2,0,1:T(2,128)(2,1)S(1)}, bf16[2,196,768]{2,0,1:T(2,128)(2,1)}, u32[]{:S(2)}) copy-start(bf16[2,196,768]{2,0,1:T(2,128)(2,1)} %param.16) | copy-start | bytes 1806340
  4.4 185.0 %copy-start.18 = (s32[2,196]{1,0:T(2,128)S(1)}, s32[2,196]{1,0:T(2,128)}, u32[]{:S(2)}) copy-start(s32[2,196]{1,0:T(2,128)} %param.18) | copy-start | bytes 4708
  187.5 2.2 copy-start.19
  193.0 0.7 copy-start
  193.7 8.5 %copy-start.9 = (bf16[2,98,768]{2,0,1:T(2,128)(2,1)S(1)}, bf16[2,98,768]{2,0,1:T(2,128)(2,1)}, u32[]{:S(2)}) copy-start(bf16[2,98,768]{2,0,1:T(2,128)(2,1)} %param.17) | copy-start | bytes 903172
  200.9 48.7 %collective-permute-start = (bf16[2,224,768]{2,1,0:T(8,128)(2,1)}, bf16[2,224,768]{2,1,0:T(8,128)(2,1)S(1)}, u32[]{:S(2)}, u32[]{:S(2)}) collective-permute-start(bf16[2,224,768]{2,1,0:T(8,128)(2,1)} %get-tuple-element.94), channel_id=1, source_target_pairs={{0,16},{1,17},{2,18},{3,19},{4,20},{5,21},{6,22},{7,23},{8,24},{9,... | collective-permute-start | bytes 2064392 | tf_op jit(solution)/shard_map/ppermute | solution.py:23
  249.6 0.9 copy-start.3
  322.9 18.5 %collective-permute-start.1 = (bf16[224,768]{1,0:T(8,128)(2,1)}, bf16[224,768]{1,0:T(8,128)(2,1)S(1)}, u32[]{:S(2)}, u32[]{:S(2)}) collective-permute-start(bf16[224,768]{1,0:T(8,128)(2,1)} %get-tuple-element.97), channel_id=1, source_target_pairs={{16,0},{17,1},{18,2},{19,3},{20,4},{21,5},{22,6},{23,7},{24,8},{25... | collective-permute-start | bytes 1032200 | tf_op jit(solution)/shard_map/ppermute | solution.py:23
  341.4 0.7 copy-start.8
  342.1 19.0 %copy-start.16 = (f32[1,3072]{1,0:T(1,128)S(1)}, f32[1,3072]{1,0:T(1,128)}, u32[]{:S(2)}) copy-start(f32[1,3072]{1,0:T(1,128)} %get-tuple-element.132) | copy-start | bytes 36868
  342.1 19.1 %copy-start.15 = (f32[16,768]{1,0:T(8,128)S(1)}, f32[16,768]{1,0:T(8,128)}, u32[]{:S(2)}) copy-start(f32[16,768]{1,0:T(8,128)} %get-tuple-element.130) | copy-start | bytes 147460
  363.0 166.1 %copy-start.1 = (f32[2,196,768]{2,1,0:T(8,128)S(1)}, f32[2,196,768]{2,1,0:T(8,128)}, u32[]{:S(2)}) copy-start(f32[2,196,768]{2,1,0:T(8,128)} %get-tuple-element.124) | copy-start | bytes 3612676
  363.0 166.1 %copy-start.2 = (f32[2,196,768]{2,1,0:T(8,128)S(1)}, f32[2,196,768]{2,1,0:T(8,128)}, u32[]{:S(2)}) copy-start(f32[2,196,768]{2,1,0:T(8,128)} %get-tuple-element.123) | copy-start | bytes 3612676
  529.3 1.7 copy-start.17
  529.3 3.7 copy-start.7
  529.3 4.4 copy-start.13
  529.3 5.1 copy-start.6
  531.0 4.3 copy-start.5
  533.7 2.3 copy-start.12
  534.4 2.3 copy-start.14
  534.4 3.0 copy-start.11
  535.2 2.9 copy-start.10

commit v3 on v2

--- a/solution.py
+++ b/solution.py
@@ -1,3 +1,4 @@
+import copy
 import functools
 
 import jax
@@ -78,115 +79,6 @@
     barrier = pltpu.get_barrier_semaphore()
     for device in devices:
         pl.semaphore_signal(barrier, inc=1, device_id=device, device_id_type=MESH_ID)
-
-
-def gather_kernel(count, groups, *refs):
-    shards_in = refs[:count]
-    wholes = refs[count : 2 * count]
-    own_sem, z_send, z_recv, y_send, y_recv, c_send, c_recv = refs[2 * count :]
-    section, index, outer, mid, core = place()
-    mid_device = (section, slot(outer, 1 - mid, core))
-    core_device = (section, slot(outer, mid, 1 - core))
-
-    def outer_device(k):
-        return (section, slot((outer + k) % groups, mid, core))
-
-    barrier = pltpu.get_barrier_semaphore()
-    greet([mid_device, core_device])
-    each(
-        groups - 1,
-        lambda k: pl.semaphore_signal(
-            barrier, inc=1, device_id=outer_device(k + 1), device_id_type=MESH_ID
-        ),
-    )
-    pl.semaphore_wait(barrier, groups + 1)
-
-    def own_copy(m):
-        return pltpu.make_async_copy(shards_in[m], wholes[m].at[index], own_sem.at[m])
-
-    def z_copy(m, k):
-        return remote(
-            shards_in[m], wholes[m].at[index], z_send.at[m, k], z_recv.at[m, k], outer_device(k)
-        )
-
-    def z_arrival(m, k):
-        origin = slot((outer - k + groups) % groups, mid, core)
-        return remote(
-            shards_in[m], wholes[m].at[origin], z_send.at[m, k], z_recv.at[m, k], outer_device(k)
-        )
-
-    def y_copy(m, k, own):
-        origin = slot((outer - k + groups) % groups, mid, core)
-        src = shards_in[m] if own else wholes[m].at[origin]
-        return remote(src, wholes[m].at[origin], y_send.at[m, k], y_recv.at[m, k], mid_device)
-
-    def y_arrival(m, k):
-        origin = slot((outer - k + groups) % groups, 1 - mid, core)
-        piece = wholes[m].at[origin]
-        return remote(piece, piece, y_send.at[m, k], y_recv.at[m, k], mid_device)
-
-    def c_copy(m, k, far, own):
-        origin = slot((outer - k + groups) % groups, 1 - mid if far else mid, core)
-        src = shards_in[m] if own else wholes[m].at[origin]
-        at = k * 2 + far
-        return remote(src, wholes[m].at[origin], c_send.at[m, at], c_recv.at[m, at], core_device)
-
-    def c_arrival(m, k, far):
-        origin = slot((outer - k + groups) % groups, 1 - mid if far else mid, 1 - core)
-        piece = wholes[m].at[origin]
-        at = k * 2 + far
-        return remote(piece, piece, c_send.at[m, at], c_recv.at[m, at], core_device)
-
-    for m in range(count):
-        each(groups - 1, lambda k: z_copy(m, k + 1).start())
-        y_copy(m, 0, True).start()
-    for m in range(count):
-        own_copy(m).start()
-        c_copy(m, 0, 0, True).start()
-    for m in range(count):
-
-        def pass_on(k):
-            z_arrival(m, k + 1).wait_recv()
-            y_copy(m, k + 1, False).start()
-            c_copy(m, k + 1, 0, False).start()
-
-        each(groups - 1, pass_on)
-    for m in range(count):
-
-        def hand_over(k):
-            y_arrival(m, k).wait_recv()
-            c_copy(m, k, 1, False).start()
-
-        each(groups, hand_over)
-    for m in range(count):
-        own_copy(m).wait()
-        each(groups - 1, lambda k: z_copy(m, k + 1).wait_send())
-
-        def finish(k):
-            y_arrival(m, k).wait_send()
-            for far in range(2):
-                c_arrival(m, k, far).wait_send()
-                c_arrival(m, k, far).wait_recv()
-
-        each(groups, finish)
-
-
-def gather_all(pieces):
-    devices = lax.axis_size("dp")
-    groups = devices // 4
-    count = len(pieces)
-    sems = [pltpu.SemaphoreType.DMA((count,))]
-    for width in (groups, groups, groups, groups, 2 * groups, 2 * groups):
-        sems.append(pltpu.SemaphoreType.DMA((count, width)))
-    return pl.pallas_call(
-        functools.partial(gather_kernel, count, groups),
-        out_shape=[jax.ShapeDtypeStruct((devices,) + p.shape, p.dtype) for p in pieces],
-        in_specs=[pl.BlockSpec(memory_space=pl.ANY)] * count,
-        out_specs=[pl.BlockSpec(memory_space=pl.ANY)] * count,
-        scratch_shapes=sems,
-        compiler_params=pltpu.CompilerParams(collective_id=1, has_side_effects=True),
-        name="gather_weights",
-    )(*pieces)
 
 
 def add_rows(target, at, other, other_at):
@@ -1126,9 +1018,390 @@
     )(returned, orders, *lead_w, *lead_small, *enc_saved, *reg_pairs)
 
 
-def exchange(pieces, own_path):
-    if own_path:
-        return gather_all(pieces)
+SMALL_ROWS = 48
+
+
+class Feed:
+    WINDOW = 3
+
+    def __init__(self, groups, shards_in, wholes, sems):
+        self.groups, self.shards, self.wholes = groups, shards_in, wholes
+        self.own, self.zs, self.zr, self.ys, self.yr, self.cs, self.cr = sems
+        self.count = len(shards_in)
+        self.section, self.index, self.outer, self.mid, self.core = place()
+        self.begun = self.at = 0
+        self.done = set()
+        self.steps = [("z", 0), ("y", 0), ("z", 1)]
+        for m in range(2, self.count):
+            self.steps += [("z", m), ("y", m - 1)]
+        self.steps.append(("y", self.count - 1))
+
+    def branch(self):
+        other = copy.copy(self)
+        other.done = set(self.done)
+        return other
+
+    def devices(self):
+        mid = (self.section, slot(self.outer, 1 - self.mid, self.core))
+        core = (self.section, slot(self.outer, self.mid, 1 - self.core))
+        return mid, core
+
+    def outer_device(self, k):
+        return (self.section, slot((self.outer + k) % self.groups, self.mid, self.core))
+
+    def origin(self, k, far=0, other_core=False):
+        outer = (self.outer - k + self.groups) % self.groups
+        mid = 1 - self.mid if far else self.mid
+        return slot(outer, mid, 1 - self.core if other_core else self.core)
+
+    def own_copy(self, m):
+        return pltpu.make_async_copy(
+            self.shards[m], self.wholes[m].at[self.index], self.own.at[m]
+        )
+
+    def z_copy(self, m, k, arrival=False):
+        at = self.origin(k) if arrival else self.index
+        return remote(
+            self.shards[m],
+            self.wholes[m].at[at],
+            self.zs.at[m, k],
+            self.zr.at[m, k],
+            self.outer_device(k),
+        )
+
+    def y_copy(self, m, k, own=False, arrival=False):
+        piece = self.wholes[m].at[self.origin(k, far=1 if arrival else 0)]
+        src = self.shards[m] if own else piece
+        return remote(src, piece, self.ys.at[m, k], self.yr.at[m, k], self.devices()[0])
+
+    def c_copy(self, m, k, far, own=False, arrival=False):
+        piece = self.wholes[m].at[self.origin(k, far, arrival)]
+        src = self.shards[m] if own else piece
+        at = k * 2 + far
+        return remote(src, piece, self.cs.at[m, at], self.cr.at[m, at], self.devices()[1])
+
+    def begin(self, upto):
+        while self.begun < min(upto, self.count):
+            m = self.begun
+            each(self.groups - 1, lambda k: self.z_copy(m, k + 1).start())
+            self.y_copy(m, 0, own=True).start()
+            self.c_copy(m, 0, 0, own=True).start()
+            self.own_copy(m).start()
+            self.begun += 1
+
+    def step(self):
+        kind, m = self.steps[self.at]
+        self.at += 1
+        if kind == "z":
+
+            def pass_on(k):
+                self.z_copy(m, k + 1, arrival=True).wait_recv()
+                self.y_copy(m, k + 1).start()
+                self.c_copy(m, k + 1, 0).start()
+
+            each(self.groups - 1, pass_on)
+            self.begin(m + 1 + self.WINDOW)
+        else:
+
+            def hand_over(k):
+                self.y_copy(m, k, arrival=True).wait_recv()
+                self.c_copy(m, k, 1).start()
+
+            each(self.groups, hand_over)
+
+    def pump(self, kind, m):
+        while (kind, m) in self.steps[self.at :]:
+            self.step()
+
+    def need(self, m):
+        self.pump("y", m)
+        if m in self.done:
+            return
+        self.done.add(m)
+
+        def last(k):
+            for far in range(2):
+                self.c_copy(m, k, far, arrival=True).wait_recv()
+
+        each(self.groups, last)
+        self.own_copy(m).wait()
+
+    def drain(self):
+        for m in range(self.count):
+            self.need(m)
+            each(self.groups - 1, lambda k: self.z_copy(m, k + 1).wait_send())
+
+            def finish_sends(k):
+                self.y_copy(m, k).wait_send()
+                for far in range(2):
+                    self.c_copy(m, k, far).wait_send()
+
+            each(self.groups, finish_sends)
+
+
+class FedSlots(Slots):
+    def __init__(self, places, sems, feed):
+        super().__init__(places, sems)
+        self.feed = feed
+        self.started = [False] * len(places)
+
+    def plan(self, m, piece):
+        self.queue[m].append(piece)
+
+    def fetch(self, m):
+        if not self.started[m] and self.queue[m]:
+            piece = self.queue[m][0]
+            self.feed.need(piece)
+            self.copy(m, self.feed.flat[piece]).start()
+            self.started[m] = True
+
+    def open(self, m):
+        self.fetch(m)
+        if not self.ready[m]:
+            self.copy(m, self.feed.flat[self.queue[m][0]]).wait()
+            self.ready[m] = True
+        return self.places[m]
+
+    def close(self, m):
+        self.queue[m].pop(0)
+        self.ready[m] = self.started[m] = False
+        if self.queue[m] and self.queue[m][0] in self.feed.done:
+            self.fetch(m)
+
+
+def unpack_small(small, devices, lead_vec, lead_bias, side_vec, side_bias):
+    width = D // devices
+    per = FF // devices // width
+    for d in range(devices):
+        lanes = slice(d * width, d * width + width)
+        block = small[d].astype(HIGH)
+        lead_vec[0:16, lanes] = block[0:16, 0:width]
+        side_vec[0:16, lanes] = block[16:32, 0:width]
+        for i in range(per):
+            first = (d * per + i) * width
+            lead_bias[0:1, first : first + width] = block[32 + i : 33 + i, 0:width]
+            side_bias[0:1, first : first + width] = block[40 + i : 41 + i, 0:width]
+
+
+def pack_small(lead_vectors, lead_bias, side_vectors, side_bias):
+    width = lead_vectors.shape[1]
+
+    def block(rows, height):
+        rows = rows.reshape(-1, width)
+        return jnp.pad(rows, ((0, height - rows.shape[0]), (0, 128 - width)))
+
+    return jnp.concatenate(
+        [block(lead_vectors, 16), block(side_vectors, 16), block(lead_bias, 8), block(side_bias, 8)]
+    )
+
+
+def layer_kernel(crops, devices, *refs):
+    refs = list(refs)
+
+    def grab(n):
+        taken = refs[:n]
+        del refs[:n]
+        return taken
+
+    def named(names):
+        return dict(zip(names, grab(len(names))))
+
+    shards_in = grab(9)
+    patches, orders, pos, cotangent = grab(4)
+    wholes = grab(9)
+    rows_out, lead_vec_grad, lead_bias_grad, dec_vec_grad, dec_bias_grad = grab(5)
+    own, reg = named(OUT_DEC), named(OUT_REG)
+    own.update(named(KEEP_DEC))
+    reg.update(named(KEEP_REG))
+    places = grab(4)
+    lead_vec, lead_bias, side_vec, side_bias, small = grab(5)
+    stream, context, resid, regressed, grad, temp, pos_visible, pos_masked = grab(8)
+    low_temp, first_pack, second_pack = grab(3)
+    sems, small_sem, x_send, x_recv = grab(4)
+    groups = devices // 4
+    feed = Feed(groups, shards_in, wholes, refs)
+    feed.flat = [None] + [
+        w.reshape(devices * w.shape[1], w.shape[2]) for w in wholes[1:]
+    ]
+    section = feed.section
+    tokens = crops * ROWS
+    x_device = (1 - section, feed.index)
+    greet([*feed.devices(), x_device])
+    barrier = pltpu.get_barrier_semaphore()
+    each(
+        groups - 1,
+        lambda k: pl.semaphore_signal(
+            barrier, inc=1, device_id=feed.outer_device(k + 1), device_id_type=MESH_ID
+        ),
+    )
+    pl.semaphore_wait(barrier, groups + 2)
+    feed.begin(Feed.WINDOW)
+
+    def x_copy(n):
+        piece = (first_pack.at[0], first_pack.at[1], second_pack)[n]
+        return remote(piece, piece, x_send.at[n], x_recv.at[n], x_device)
+
+    def vectors_in(feed):
+        feed.need(0)
+        fetched = pltpu.make_async_copy(wholes[0], small, small_sem)
+        fetched.start()
+        fetched.wait()
+        unpack_small(small, devices, lead_vec, lead_bias, side_vec, side_bias)
+
+    def slots_of(feed):
+        slots = FedSlots(places, sems, feed)
+        for base in (1, 5, 1):
+            for m in range(4):
+                slots.plan(m, base + m)
+        return slots
+
+    start = feed
+
+    @pl.when(section == 0)
+    def _():
+        feed = start.branch()
+        slots = slots_of(feed)
+        for kind, vec, bias, keep in ((0, lead_vec, lead_bias, own), (1, side_vec, side_bias, reg)):
+            for c in range(crops):
+                stream[crop_rows(c), :] = dot(one_hot(orders, kind, c), patches[c])
+            if kind == 0:
+                vectors_in(feed)
+            else:
+                names = ("normed", "qkv", "mixed", "second", "hidden")
+                keep = {n: reg[n] for n in names}
+            block_forward(keep, stream, None, resid, slots, vec, bias, regressed)
+            first_pack[kind] = regressed[...].astype(LOW)
+            x_copy(kind).start()
+        x_copy(2).wait_recv()
+        grad[...] = second_pack[...].astype(HIGH)
+        block_backward(
+            own, grad, temp, low_temp, slots, lead_vec, lead_vec_grad, lead_bias_grad, False, None
+        )
+        for c in range(crops):
+            rest = grad[crop_rows(c), :]
+            pick = one_hot(orders, 0, c)
+            total = jnp.zeros((PATCHES, D), HIGH)
+            for _ in range(3):
+                part = rest.astype(LOW)
+                rest = rest - part.astype(HIGH)
+                total = total + dot_tn(pick, part)
+            rows_out[c] = total
+        for n in range(2):
+            x_copy(n).wait_send()
+        feed.drain()
+
+    @pl.when(section == 1)
+    def _():
+        feed = start.branch()
+        slots = slots_of(feed)
+        for kind, place_of in enumerate((pos_visible, pos_masked)):
+            for c in range(crops):
+                pick = one_hot(orders, kind, c)
+                place_of[crop_rows(c), :] = sum(dot(pick, pos[t]) for t in (2, 1, 0))
+        vectors_in(feed)
+        stream[...] = side_vec[12:13, :] + pos_masked[...]
+        for m in range(4):
+            slots.fetch(m)
+        feed.pump("z", 5)
+        x_copy(0).wait_recv()
+        context[...] = first_pack[0].astype(HIGH) + pos_visible[...]
+        block_forward(reg, stream, context, resid, slots, lead_vec, lead_bias, regressed)
+        stream[...] = regressed[...] + pos_masked[...]
+        block_forward(own, stream, None, resid, Held(slots), side_vec, side_bias, temp)
+        for c in range(crops):
+            first = c * ROWS
+            rows_out[c, 0:MASKED, :] = regressed[first : first + MASKED, :]
+            rows_out[c, MASKED : 2 * MASKED, :] = temp[first : first + MASKED, :]
+            grad[first : first + ROWS, :] = jnp.zeros((ROWS, D), HIGH)
+            grad[first : first + MASKED, :] = cotangent[c].astype(HIGH)
+        block_backward(
+            own, grad, temp, low_temp, slots, side_vec, dec_vec_grad, dec_bias_grad, False, None
+        )
+        x_copy(1).wait_recv()
+        inside = lax.broadcasted_iota(jnp.int32, (ROWS, D), 0) < MASKED
+        for c in range(crops):
+            here = crop_rows(c)
+            apart = regressed[here, :] - first_pack[1, here, :].astype(HIGH)
+            grad[here, :] = grad[here, :] + jnp.where(inside, apart, 0.0)
+        block_backward(
+            reg, grad, temp, low_temp, slots, lead_vec, lead_vec_grad, lead_bias_grad, True, context
+        )
+        second_pack[...] = context[...].astype(LOW)
+        x_copy(2).start()
+        dec_vec_grad[12:13, :] = jnp.sum(grad[...], axis=0, keepdims=True)
+        feed.drain()
+        x_copy(2).wait_send()
+
+
+def layer(crops, devices, pieces, patches, orders, pos, cotangent):
+    tokens = crops * ROWS
+    groups = devices // 4
+    inside = [((crops, PATCHES, D), HIGH)] + SMALL_SHAPES * 2
+    inside += [save_shape(n, tokens) for n in OUT_DEC + OUT_REG]
+    scratch = places_for([save_shape(n, tokens) for n in KEEP_DEC + KEEP_REG])
+    scratch += places_for(WEIGHT_SHAPES + SMALL_SHAPES * 2)
+    scratch += places_for([((devices, SMALL_ROWS, 128), LOW)])
+    scratch += places_for([((tokens, D), HIGH)] * 8)
+    scratch += places_for([((tokens, D), LOW), ((2, tokens, D), LOW), ((tokens, D), LOW)])
+    scratch += [pltpu.SemaphoreType.DMA(s) for s in ((4,), (), (3,), (3,))]
+    scratch += [pltpu.SemaphoreType.DMA((9,))]
+    for width in (groups, groups, groups, groups, 2 * groups, 2 * groups):
+        scratch.append(pltpu.SemaphoreType.DMA((9, width)))
+    wholes = [((devices,) + p.shape, p.dtype) for p in pieces]
+    return pl.pallas_call(
+        functools.partial(layer_kernel, crops, devices),
+        out_shape=specs(wholes + inside),
+        in_specs=[ANYWHERE] * 9 + [INSIDE] * 4,
+        out_specs=[ANYWHERE] * 9 + [INSIDE] * len(inside),
+        scratch_shapes=scratch,
+        compiler_params=pltpu.CompilerParams(
+            collective_id=1, has_side_effects=True, vmem_limit_bytes=60 << 20
+        ),
+        name="layer",
+    )(*pieces, patches, orders, pos, cotangent)
+
+
+def lead_weights_kernel(*refs):
+    refs = list(refs)
+    own, reg = dict(zip(OUT_DEC, refs[:8])), dict(zip(OUT_REG, refs[8:18]))
+    outs, scratch, (place_a, place_c, sems) = refs[18:22], refs[22:26], refs[26:]
+
+    def weights_of(pairs, joined):
+        for m in (3, 2, 1, 0):
+            left, right = PAIRS[m]
+            rows = pairs[left].shape[1]
+            extra = (pairs["normed_c"], pairs["dkv_c"], place_c) if joined and m == 0 else None
+            weight_grad(
+                scratch[m], pairs[left], pairs[right], place_a.at[0:rows, :], 0, extra, D
+            )
+            ship(m, scratch, outs, sems).start()
+        for m in range(4):
+            ship(m, scratch, outs, sems).wait()
+
+    @pl.when(lax.axis_index("section") == 0)
+    def _():
+        weights_of(own, False)
+
+    @pl.when(lax.axis_index("section") == 1)
+    def _():
+        weights_of(reg, True)
+
+
+def lead_weights(crops, own_pairs, reg_pairs):
+    tokens = crops * ROWS
+    return pl.pallas_call(
+        lead_weights_kernel,
+        out_shape=specs(WEIGHT_SHAPES),
+        in_specs=[INSIDE] * 18,
+        out_specs=[ANYWHERE] * 4,
+        scratch_shapes=places_for(WEIGHT_SHAPES + [((FF, tokens), LOW), ((D, tokens), LOW)])
+        + [pltpu.SemaphoreType.DMA((4,))],
+        compiler_params=params(),
+        name="lead_weights",
+    )(*own_pairs, *reg_pairs)
+
+
+def exchange(pieces):
     return [lax.all_gather(p, "dp", axis=0) for p in pieces]
 
 
@@ -1203,6 +1476,49 @@
     return lead_out[:4] + [lead_vectors, lead_bias], dec_out[:4] + [dec_vectors, dec_bias]
 
 
+def run_fused(crops, devices, patches, cotangent, orders, lead, side, smalls):
+    pieces = [pack_small(*smalls)] + lead + side
+    outs = layer(crops, devices, pieces, patches, orders, position_parts(), cotangent)
+    rows, vec, bias, dec_vec, dec_bias, *pairs = outs[9:]
+    own_pairs, reg_pairs = pairs[: len(OUT_DEC)], pairs[len(OUT_DEC) :]
+    dec_big = decoder_weights(crops, own_pairs, devices, True)
+    lead_big = lead_weights(crops, own_pairs, reg_pairs)
+    return rows, lead_big, (vec[:12], bias[0]), dec_big, (dec_vec[:13], dec_bias[0])
+
+
+def run_apart(crops, devices, patches, cotangent, orders, lead, side, smalls):
+    on_encoder = lax.axis_index("section") == 0
+    wholes = exchange(lead + side + [as_small(smalls, 16)])
+    big = [w.reshape(-1, w.shape[2]) for w in wholes[:8]]
+    flat = wholes[8].reshape(devices, -1).astype(jnp.float32)
+    lv, lb, sv, sb = take_flat(flat, [p.shape for p in smalls])
+
+    def sixteen(vectors):
+        rows = spread_columns(vectors)
+        return jnp.pad(rows, ((0, 16 - rows.shape[0]), (0, 0)))
+
+    lead_w, side_w = big[:4], big[4:]
+    lead_small = [sixteen(lv), lb.reshape(1, -1)]
+    all_small = lead_small + [sixteen(sv), sb.reshape(1, -1)]
+    pack, pos_visible, pos_masked, *enc_saved = encode(
+        crops, patches, orders, position_parts(), lead_w, side_w, all_small
+    )
+    arrived = passed_along(pack, "section", 1)
+    grad_latents, latent_rows, reg_vec, reg_bias, dec_vec, dec_bias, *pairs = regress(
+        crops, arrived, pos_visible, pos_masked, cotangent, lead_w, side_w, all_small
+    )
+    reg_pairs, dec_pairs = pairs[: len(OUT_REG)], pairs[len(OUT_REG) :]
+    returned = passed_along(grad_latents, "section", -1)
+    dec_big = decoder_weights(crops, dec_pairs, devices, False)
+    *lead_big, grad_rows, enc_vec, enc_bias = finish(
+        crops, returned, orders, lead_w, lead_small, enc_saved, reg_pairs
+    )
+    vec = jnp.where(on_encoder, enc_vec, reg_vec)[:12]
+    bias = jnp.where(on_encoder, enc_bias, reg_bias)
+    rows = jnp.where(on_encoder, grad_rows, latent_rows)
+    return rows, lead_big, (vec, bias[0]), dec_big, (dec_vec[:13], dec_bias[0])
+
+
 def padded_orders(ordering, part):
     cut = ordering[:, MASKED:] if part == 0 else ordering[:, :MASKED]
     cut = jnp.pad(cut, ((0, 0), (0, ROWS - MASKED)), constant_values=-1)
@@ -1226,48 +1542,18 @@
     side_vectors,
     side_bias,
 ):
-    on_encoder = lax.axis_index("section") == 0
     devices = lax.axis_size("dp")
-    own_path = devices % 4 == 0 and lead_qkv.shape[1] % 16 == 0
     crops = patches.shape[0]
-    small = as_small([lead_vectors[0], lead_bias[0], side_vectors[0], side_bias[0]], 16)
-    pieces = [lead_qkv[0], lead_proj[0], lead_up[0], lead_down[0]]
-    pieces += [side_qkv[0], side_proj[0], side_up[0], side_down[0], small]
-    wholes = exchange(pieces, own_path)
-    big = [w.reshape(-1, w.shape[2]) for w in wholes[:8]]
-    flat = wholes[8].reshape(devices, -1).astype(jnp.float32)
-    lv, lb, sv, sb = take_flat(
-        flat,
-        [lead_vectors.shape[1:], lead_bias.shape[1:], side_vectors.shape[1:], side_bias.shape[1:]],
+    orders = jnp.stack([padded_orders(ordering, 0), padded_orders(ordering, 1)])
+    lead = [lead_qkv[0], lead_proj[0], lead_up[0], lead_down[0]]
+    side = [side_qkv[0], side_proj[0], side_up[0], side_down[0]]
+    smalls = [lead_vectors[0], lead_bias[0], side_vectors[0], side_bias[0]]
+    own_path = devices % 4 == 0 and lead[0].shape[0] % 16 == 0
+    run = run_fused if own_path else run_apart
+    rows, lead_big, lead_small, dec_big, dec_small = run(
+        crops, devices, patches, cotangent, orders, lead, side, smalls
     )
-
-    def sixteen(vectors):
-        rows = spread_columns(vectors)
-        return jnp.pad(rows, ((0, 16 - rows.shape[0]), (0, 0)))
-
-    lead_w, side_w = big[:4], big[4:]
-    lead_small = [sixteen(lv), lb.reshape(1, -1)]
-    smalls = lead_small + [sixteen(sv), sb.reshape(1, -1)]
-    orders = jnp.stack([padded_orders(ordering, 0), padded_orders(ordering, 1)])
-    pack, pos_visible, pos_masked, *enc_saved = encode(
-        crops, patches, orders, position_parts(), lead_w, side_w, smalls
-    )
-    arrived = passed_along(pack, "section", 1)
-    grad_latents, latent_rows, reg_vec, reg_bias, dec_vec, dec_bias, *pairs = regress(
-        crops, arrived, pos_visible, pos_masked, cotangent, lead_w, side_w, smalls
-    )
-    reg_pairs, dec_pairs = pairs[: len(OUT_REG)], pairs[len(OUT_REG) :]
-    returned = passed_along(grad_latents, "section", -1)
-    dec_big = decoder_weights(crops, dec_pairs, devices, own_path)
-    *lead_big, grad_rows, enc_vec, enc_bias = finish(
-        crops, returned, orders, lead_w, lead_small, enc_saved, reg_pairs
-    )
-    vec = jnp.where(on_encoder, enc_vec, reg_vec)[:12]
-    bias = jnp.where(on_encoder, enc_bias, reg_bias)
-    lead_out, dec_out = total_grads(
-        lead_big, (vec, bias[0]), dec_big, (dec_vec[:13], dec_bias[0]), own_path
-    )
-    rows = jnp.where(on_encoder, grad_rows, latent_rows)
+    lead_out, dec_out = total_grads(lead_big, lead_small, dec_big, dec_small, own_path)
     return (rows[None],) + tuple(o[None] for o in lead_out) + tuple(dec_out)
 
 

time: 547 us -> 489 us (0.89)
  waiting for transfers between devices: 46.7 us -> 0 us
  Pallas kernels: 459 us -> 450 us
    ppermute x2 -> x0, waiting for transfers between devices: 46.7 us -> none  [passed_along(): return lax.ppermute(array, axis, pairs)]
    pallas_call x4 -> x2, Pallas kernels: 282 us -> 260 us  [the longest x1 244 us: layer(): pl.pallas_call(functools.partial(layer_kernel, crops, devices), out_shape...]
    pallas_call x1, Pallas kernels: 164 us -> 176 us  [reduce_all(): pl.pallas_call(functools.partial(reduce_kernel, nl, nd, groups, None), ou...]
    unnamed x55 -> x35, local copies, waits for them, and re-layouts: 13.6 us -> 14.4 us
  transfers between devices with their start and end apart: 2 -> 0, of which waited for: 1 -> 0; matrix products, arithmetic and copies ran while one was open for 1% -> 0% of each run, Pallas kernels for 2% -> 0%
where the time goes in v3:
time: 489 us; the launch traced here: 479 us
  Pallas kernels  450 us (92%)
  local copies, waits for them, and re-layouts  22.4 us (5%)
  other arithmetic  5.63 us (1%)
    pallas_call x1, Pallas kernels, layer(): pl.pallas_call(functools.partial(layer_kernel, crops, devices), out_shape...  244 us
    pallas_call x1, Pallas kernels, reduce_all(): pl.pallas_call(functools.partial(reduce_kernel, nl, nd, groups, None), ou...  176 us
    pallas_call x1, Pallas kernels, lead_weights(): pl.pallas_call(lead_weights_kernel, out_shape=specs(WEIGHT_SHAPES), in_sp...  16 us
    unnamed x35, local copies, waits for them, and re-layouts  14.4 us
    pallas_call x1, Pallas kernels, decoder_weights(): pl.pallas_call(functools.partial(decoder_weights_kernel, stacks), out_sha...  13.3 us

profile of v3, /device:TPU:3, one launch (start us, length us, event | category | flops | bytes accessed | tf_op | source)
XLA Modules:
  0.0 479.2 jit_solution(16507649526995982707)
XLA Ops:
  0.6 2.0 copy.54.refs_9_
  2.6 0.8 slice.25
  3.5 0.7 slice_select_fusion
  4.4 0.7 pad_add_fusion.refs_10_
  5.1 1.7 copy.55.refs_12_
  6.9 0.7 reduce
  7.6 0.7 reduce.1
  8.4 1.3 fusion.9.refs_0_
  9.7 244.4 %layer.1 = (bf16[16,48,128]{2,1,0:T(8,128)(2,1)}, bf16[16,48,2304]{2,1,0:T(8,128)(2,1)}, bf16[16,48,768]{2,1,0:T(8,128)(2,1)}, bf16[16,48,3072]{2,1,0:T(8,128)(2...) custom-call(bf16[48,128]{1,0:T(8,128)(2,1)} %fusion.9.refs_0_, ...), custom_call_target="tpu_custom_call" | custom-call | tf_op jit(solution)/shard_map/layer/pallas_call | solution.py:1351
  254.1 13.3 %decoder_weights.1 = (bf16[32,48,1152]{2,1,0:T(8,128)(2,1)}, bf16[32,48,384]{2,1,0:T(8,128)(2,1)}, bf16[32,48,1536]{2,1,0:T(8,128)(2,1)}, bf16[3072,768]{1,0:T(8,128)(2,1)}) custom-call(bf16[224,768]{1,0:T(8,128)(2,1)} %get-tuple-element.55.refs_0_, bf16[224,2304]{1,0:T(8,128)(2,1)} %get-tuple-element.56.refs_1_, ...), custom_call_target="tpu_custom_call" | custom-call | tf_op jit(solution)/shard_map/decoder_weights/pallas_call | solution.py:989
  267.5 16.0 %lead_weights.1 = (bf16[768,2304]{1,0:T(8,128)(2,1)}, bf16[768,768]{1,0:T(8,128)(2,1)}, bf16[768,3072]{1,0:T(8,128)(2,1)}, bf16[3072,768]{1,0:T(8,128)(2,1)}) custom-call(bf16[224,768]{1,0:T(8,128)(2,1)} %get-tuple-element.55.refs_0_, bf16[224,2304]{1,0:T(8,128)(2,1)} %get-tuple-element.56.refs_1_, bf16[224,768]{1,0:T(8,128)(2,1)} %get-tuple-element.57.refs_2_, ...), custom_call_target="tpu_custom_call" | custom-call | tf_op jit(solution)/shard_map/lead_weights/pallas_call | solution.py:1392
  285.2 0.7 copy.61
  287.6 176.4 %reduce_grads.1 = (f32[48,2304]{1,0:T(8,128)}, f32[48,768]{1,0:T(8,128)}, f32[48,3072]{1,0:T(8,128)}, f32[192,768]{1,0:T(8,128)}, f32[8,128]{1,0:T(8,128)}, /*in...) custom-call(bf16[16,48,2304]{2,1,0:T(8,128)(2,1)} %bitcast.46, ...), custom_call_target="tpu_custom_call" | custom-call | tf_op jit(solution)/shard_map/reduce_grads/pallas_call | solution.py:300
  464.1 0.8 slice.31
  465.6 1.4 broadcast_in_dim_reshape.3
  467.0 1.3 slice.30
  468.3 1.3 slice.32
  469.5 1.6 copy.59
  471.2 1.8 copy.72
  473.0 1.6 copy.73
  474.6 0.8 copy.74
  475.4 0.8 copy.75
  477.5 0.7 copy.78
  478.3 0.7 copy.79
  (44 shorter events, 6.0 us)
Async XLA Ops:
  267.5 16.5 %copy-start.10 = (f32[1,3072]{1,0:T(1,128)S(1)}, f32[1,3072]{1,0:T(1,128)}, u32[]{:S(2)}) copy-start(f32[1,3072]{1,0:T(1,128)} %get-tuple-element.84) | copy-start | bytes 36868
  267.5 17.3 %copy-start.7 = (f32[16,768]{1,0:T(8,128)S(1)}, f32[16,768]{1,0:T(8,128)}, u32[]{:S(2)}) copy-start(f32[16,768]{1,0:T(8,128)} %get-tuple-element.83) | copy-start | bytes 147460
  267.5 18.4 %copy-start.9 = (f32[1,3072]{1,0:T(1,128)S(1)}, f32[1,3072]{1,0:T(1,128)}, u32[]{:S(2)}) copy-start(f32[1,3072]{1,0:T(1,128)} %get-tuple-element.78) | copy-start | bytes 36868
  267.5 19.2 %copy-start.8 = (f32[16,768]{1,0:T(8,128)S(1)}, f32[16,768]{1,0:T(8,128)}, u32[]{:S(2)}) copy-start(f32[16,768]{1,0:T(8,128)} %get-tuple-element.77) | copy-start | bytes 147460
  287.6 181.9 %copy-start = (f32[2,196,768]{2,1,0:T(8,128)S(1)}, f32[2,196,768]{2,1,0:T(8,128)}, u32[]{:S(2)}) copy-start(f32[2,196,768]{2,1,0:T(8,128)} %get-tuple-element.54) | copy-start | bytes 3612676
  464.1 10.5 %copy-start.2 = (f32[48,3072]{1,0:T(8,128)S(1)}, f32[48,3072]{1,0:T(8,128)}, u32[]{:S(2)}) copy-start(f32[48,3072]{1,0:T(8,128)} %get-tuple-element.87) | copy-start | bytes 1769476
  464.1 11.3 %copy-start.1 = (f32[192,768]{1,0:T(8,128)S(1)}, f32[192,768]{1,0:T(8,128)}, u32[]{:S(2)}) copy-start(f32[192,768]{1,0:T(8,128)} %get-tuple-element.88) | copy-start | bytes 1769476
  464.1 12.1 %copy-start.5 = (f32[24,2304]{1,0:T(8,128)S(1)}, f32[24,2304]{1,0:T(8,128)}, u32[]{:S(2)}) copy-start(f32[24,2304]{1,0:T(8,128)} %get-tuple-element.167) | copy-start | bytes 663556
  464.1 12.8 %copy-start.6 = (f32[24,768]{1,0:T(8,128)S(1)}, f32[24,768]{1,0:T(8,128)}, u32[]{:S(2)}) copy-start(f32[24,768]{1,0:T(8,128)} %get-tuple-element.168) | copy-start | bytes 221188
  464.1 13.4 %copy-start.4 = (f32[24,3072]{1,0:T(8,128)S(1)}, f32[24,3072]{1,0:T(8,128)}, u32[]{:S(2)}) copy-start(f32[24,3072]{1,0:T(8,128)} %get-tuple-element.169) | copy-start | bytes 884740
  469.5 8.7 %copy-start.3 = (f32[96,768]{1,0:T(8,128)S(1)}, f32[96,768]{1,0:T(8,128)}, u32[]{:S(2)}) copy-start(f32[96,768]{1,0:T(8,128)} %get-tuple-element.170) | copy-start | bytes 884740
